TPU v7x, 128 devices: a whole 4x4x4 slice. The times are simulated.
128 devices in a mesh: dp: 8 (over x, core), tensor: 16 (over y, z).
Axes of the slice: x: 4, y: 4, z: 4, core: 2. Of those that a mesh axis runs over, the one named last changes fastest.
Arguments:
- gradients: bfloat16 [8, 3, 2, 8192, 1024], P('dp', None, None, 'tensor'), may hold values from -60 to 60
- memory: bfloat16 [8, 3, 2, 8192, 1024], P('dp', None, None, 'tensor'), may hold values from -4 to 4
- initial_query: float32 [3, 2, 1024, 64], replicated, may hold values from -0.1875 to 0.1875
Outputs:
- new_memory: bfloat16 [8, 3, 2, 8192, 1024], P('dp', None, None, 'tensor')
- decompressed: bfloat16 [3, 2, 8192, 1024], P(None, None, 'tensor')
- updated_query_factor: float32 [3, 2, 1024, 64], replicated
All inputs are finite; a program needn't handle non-finite values.
Results may differ from a plain program's by a relative error of at most 0.012.
Values may be sent and summed in bfloat16 or wider, within the bound.
A program may use at most 128 MiB of HBM per device.

v0:
```python
import jax
import jax.numpy as jnp
from jax import lax
from jax.sharding import PartitionSpec as P


def orthonormal_basis(matrix_rows, gram_product):
    factor = jnp.linalg.cholesky(gram_product)
    return lax.linalg.triangular_solve(
        factor, matrix_rows, left_side=False, lower=True, transpose_a=True
    )


def local_gram(matrix_rows):
    return jnp.einsum("wotc,wotj->wocj", matrix_rows, matrix_rows, precision=lax.Precision.HIGHEST)


def body(gradients, memory, initial_query):
    replicas = lax.axis_size("dp")
    merged = (gradients[0].astype(jnp.float32) + memory[0].astype(jnp.float32)).astype(jnp.bfloat16)
    query_low = initial_query.astype(jnp.bfloat16)
    partial_value_product = jnp.einsum(
        "lmdk,lmkr->lmdr", merged, query_low, preferred_element_type=jnp.float32
    )
    summed = lax.psum(partial_value_product, "dp")
    gram_product = lax.psum(local_gram(summed), "tensor")
    basis = orthonormal_basis(summed, gram_product).astype(jnp.bfloat16)
    projected = jnp.einsum("lmdk,lmdr->lmkr", merged, basis, preferred_element_type=jnp.float32)
    query_whole = lax.psum(projected, ("dp", "tensor"))
    updated_query_factor = query_whole / replicas
    query_next_low = updated_query_factor.astype(jnp.bfloat16)
    rebuilt = jnp.einsum(
        "lmdr,lmkr->lmdk", basis, query_next_low, preferred_element_type=jnp.float32
    )
    new_memory = (merged.astype(jnp.float32) - rebuilt).astype(jnp.bfloat16)
    return (new_memory[None], rebuilt.astype(jnp.bfloat16), updated_query_factor)


def solution(mesh):
    in_specs = (P("dp", None, None, "tensor", None), P("dp", None, None, "tensor", None), P())
    out_specs = (P("dp", None, None, "tensor", None), P(None, None, "tensor", None), P())
    return jax.shard_map(body, mesh=mesh, in_specs=in_specs, out_specs=out_specs, check_vma=False)
```

profile of v0, /device:TPU:1, one launch (start us, length us, event | category | flops | bytes accessed | tf_op | source)
XLA Modules:
  0.0 409.2 jit_solution(9929841376307400647)
XLA Ops:
  7.2 0.0 all-reduce.4.cloned.1.call-start
  7.2 7.9 %fusion.4 = f32[3,2,512,64]{2,3,1,0:T(8,128)} fusion(f32[3,2,1024,64]{2,3,1,0:T(8,128)} %param.5, bf16[1,3,2,512,1024]{4,3,2,1,0:T(8,128)(2,1)} %param.4, bf16[1,3,2,512,1024]{4,3,2,1,0:T(8,128)(2,1)} %param.3), kind=kOutput, calls=%fused_computation.8 | convolution fusion | flops 415629312 | bytes 14942208 | tf_op jit(solution)/shard_map/lmdk,lmkr->lmdr/dot_general | solution.py:22
  15.1 0.0 all-reduce.4.cloned.1.call-update
  15.2 0.0 all-reduce.6.cloned.1.call-start
  15.2 62.8 %all-reduce.4.cloned.1.call-done = f32[3,2,512,64]{2,3,1,0:T(8,128)} async-done(((f32[3,2,512,64]{2,3,1,0:T(8,128)}), f32[3,2,512,64]{2,3,1,0:T(8,128)}) %all-reduce.4.cloned.1.call-update) | async-done | bytes 786448 | tf_op jit(solution)/shard_map/psum | solution.py:25
  78.0 2.9 fusion.14
  80.9 0.0 all-reduce.6.cloned.1.call-update
  81.0 0.0 all-reduce.8.cloned.1.call-start
  81.0 84.8 %all-reduce.6.cloned.1.call-done = f32[3,2,64,64]{2,3,1,0:T(8,128)} async-done(((f32[3,2,64,64]{2,3,1,0:T(8,128)}), f32[3,2,64,64]{2,3,1,0:T(8,128)}) %all-reduce.6.cloned.1.call-update) | async-done | bytes 98320 | tf_op jit(solution)/shard_map/psum | solution.py:26
  165.8 1.0 copy.14
  166.9 1.0 fusion.7
  167.8 35.2 %custom-call.7 = f32[3,2,64,64]{3,2,1,0:T(8,128)S(1)} custom-call(f32[3,2,64,64]{3,2,1,0:T(8,128)S(1)} %fusion.7), custom_call_target="Cholesky" | custom-call | tf_op jit(solution)/shard_map/jit(cholesky)/cholesky | solution.py:8
  203.0 0.1 compare_reduce_fusion
  203.2 0.1 select_bitcast_fusion
  203.3 29.5 %custom-call.8 = f32[3,2,1,64,64]{3,4,2,1,0:T(8,128)S(1)} custom-call(f32[3,2,1,64,64]{4,3,2,1,0:T(8,128)S(1)} %select_bitcast_fusion), custom_call_target="InvertDiagBlocksLowerTriangular" | custom-call | tf_op jit(solution)/shard_map/triangular_solve | solution.py:9
  232.8 2.0 convolution_convert_fusion
  234.8 7.6 %fusion.8 = f32[3,2,1024,64]{2,3,1,0:T(8,128)} fusion(bf16[3,2,512,64]{2,3,1,0:T(8,128)(2,1)S(1)} %convolution_convert_fusion, bf16[1,3,2,512,1024]{4,3,2,1,0:T(8,128)(2,1)} %param.4, bf16[1,3,2,512,1024]{4,3,2,1,0:T(8,128)(2,1)} %param.3), kind=kOutput, calls=%fused_computation.18 | convolution fusion | flops 415236096 | bytes 14548992 | tf_op jit(solution)/shard_map/lmdk,lmdr->lmkr/dot_general | solution.py:28
  242.4 0.0 all-reduce.8.cloned.1.call-update
  242.4 149.4 %all-reduce.8.cloned.1.call-done = f32[3,2,1024,64]{2,3,1,0:T(8,128)} async-done(((f32[3,2,1024,64]{2,3,1,0:T(8,128)}), f32[3,2,1024,64]{2,3,1,0:T(8,128)}) %all-reduce.8.cloned.1.call-update) | async-done | bytes 1572880 | tf_op jit(solution)/shard_map/psum | solution.py:29
  391.8 1.5 broadcast_multiply_fusion
  393.3 0.0 copy-start
  393.3 9.4 %fusion.11 = (bf16[3,2,512,1024]{3,2,1,0:T(8,128)(2,1)}, bf16[1,3,2,512,1024]{4,3,2,1,0:T(8,128)(2,1)}) fusion(bf16[1,3,2,512,1024]{4,3,2,1,0:T(8,128)(2,1)} %param.4, bf16[1,3,2,512,1024]{4,3,2,1,0:T(8,128)(2,1)} %param.3, bf16[3,2,512,64]{2,3,1,0:T(8,128)(2,1)S(1)} %convolution_convert_fusion, f32[3,2,1024,64]{2,3,1,0:T(8,128)S(1)} %broadcast_multiply_fusion), kind=kOutput, calls=%fused_computation.19 | convolution fusion | flops 428212224 | bytes 27131904 | tf_op jit(solution)/shard_map/lmdr,lmkr->lmdk/dot_general | solution.py:32
  402.7 0.0 copy-done
  (3 shorter events, 0.1 us)
Async XLA Ops:
  7.2 70.9 %all-reduce.4.cloned.1.call-start = ((), (), s32[]{:S(2)}) async-start(), calls=%async_computation | async-start | bytes 1572864 | tf_op jit(solution)/shard_map/psum | solution.py:25
  15.2 150.7 %all-reduce.6.cloned.1.call-start = ((), (), s32[]{:S(2)}) async-start(), calls=%async_computation.1 | async-start | bytes 393216 | tf_op jit(solution)/shard_map/psum | solution.py:26
  81.0 310.8 %all-reduce.8.cloned.1.call-start = ((), (), s32[]{:S(2)}) async-start(), calls=%async_computation.2 | async-start | bytes 3145728 | tf_op jit(solution)/shard_map/psum | solution.py:29
  393.3 9.4 %copy-start = (f32[3,2,1024,64]{2,3,1,0:T(8,128)}, f32[3,2,1024,64]{2,3,1,0:T(8,128)S(1)}, u32[]{:S(2)}) copy-start(f32[3,2,1024,64]{2,3,1,0:T(8,128)S(1)} %broadcast_multiply_fusion) | copy-start | bytes 4718596
Sparse Core Ops, SparseCore 0:
  15.3 62.7 all-reduce.3
  82.1 83.6 all-reduce.5
  242.5 149.2 all-reduce.7
where the time goes:
time: 409 us
  waiting for transfers between devices  297 us (73%)
  other arithmetic  67.5 us (17%)
  matrix products  29.7 us (7%)
  between operations  13.8 us (3%)
    psum x1, waiting for transfers between devices, body(): query_whole = lax.psum(projected, ('dp', 'tensor'))  149 us
    psum x1, waiting for transfers between devices, body(): gram_product = lax.psum(local_gram(summed), 'tensor')  84.8 us
    psum x1, waiting for transfers between devices, body(): summed = lax.psum(partial_value_product, 'dp')  62.8 us
    another operation x4, other arithmetic, orthonormal_basis(): factor = jnp.linalg.cholesky(gram_product)  35.4 us
    another operation x3, other arithmetic, orthonormal_basis(): lax.linalg.triangular_solve(factor, matrix_rows, left_side=False, lower=T...  29.6 us
    dot_general x1, matrix products, body(): jnp.einsum('lmdr,lmkr->lmdk', basis, query_next_low, preferred_element_ty...  9.36 us
  transfers between devices with their start and end apart: 3, of which 3 were waited for; matrix products, arithmetic and copies ran while one was open for 0% of the time, Pallas kernels for 0%

commit v1 on v0

v1 whole, which is shorter than its diff:
```python
import functools

import jax
import jax.numpy as jnp
from jax import lax
from jax.experimental import pallas as pl
from jax.experimental.pallas import tpu as pltpu
from jax.sharding import PartitionSpec as P

MESH = pl.DeviceIdType.MESH
F32 = jnp.float32
BF16 = jnp.bfloat16
LAYERS = 3
ROWS = 512
KVW = 1024
R = 64
NT = (((1,), (1,)), ((), ()))


def reduce_kernel(
    g_hbm, m_hbm, query_ref,
    merged, basis, w_all, linv,
    g_buf, m_buf, qpad, p_own, p_send, p_recv, x_slots, s_full, s_t,
    w_own, w_send, w_recv, w_sum, r1, s1, r2, e_slots, gram_y, gram_z, aug, linv_mine,
    load_sem, core_send, core_recv, x_send, x_recv, ax_send, ax_recv, gram_send, gram_recv,
):
    dp = lax.axis_index("dp")
    tensor = lax.axis_index("tensor")
    core = dp % 2
    coord = (dp // 2, tensor // 4, tensor % 4)

    def along(axis, k):
        c = [coord[0], coord[1], coord[2]]
        c[axis] = (c[axis] + k) % 4
        return (c[0] * 2 + core, c[1] * 4 + c[2])

    sibling = (dp + 1 - 2 * core, tensor)

    loads = []
    for l in range(LAYERS):
        for m in range(2):
            a = pltpu.make_async_copy(g_hbm.at[0, l, m], g_buf.at[l, m], load_sem.at[l, m, 0])
            b = pltpu.make_async_copy(m_hbm.at[0, l, m], m_buf.at[l, m], load_sem.at[l, m, 1])
            a.start()
            b.start()
            loads.append((a, b))

    barrier = pltpu.get_barrier_semaphore()
    pl.semaphore_signal(barrier, inc=1, device_id=sibling, device_id_type=MESH)
    for axis in range(3):
        for k in (1, 2, 3):
            pl.semaphore_signal(barrier, inc=1, device_id=along(axis, k), device_id_type=MESH)

    for l in range(LAYERS):
        for m in range(2):
            qpad[l, m, R * m:R * m + R, :] = query_ref[l, m].astype(BF16)
            qpad[l, m, R - R * m:2 * R - R * m, :] = jnp.zeros((R, KVW), BF16)

    sends = []

    def remote(src, dst, send_sem, recv_sem, device):
        c = pltpu.make_async_remote_copy(src, dst, send_sem, recv_sem, device_id=device, device_id_type=MESH)
        c.start()
        sends.append(c)
        return c

    half = ROWS // 2
    pc, xc, sc, wc = {}, {}, {}, {}

    def stage_a(l):
        total = None
        for m in range(2):
            a, b = loads[2 * l + m]
            a.wait()
            b.wait()
            merged[l, m] = (g_buf[l, m].astype(F32) + m_buf[l, m].astype(F32)).astype(BF16)
            part = lax.dot_general(merged[l, m], qpad[l, m], NT, preferred_element_type=F32)
            total = part if total is None else total + part
        p_own[l] = total
        p_send[l] = p_own[l, pl.ds(pl.multiple_of(half * (1 - core), half), half), :].astype(BF16)
        if l == 0:
            pl.semaphore_wait(barrier, 10)
        pc[l] = remote(p_send.at[l], p_recv.at[l], core_send.at[l, 0], core_recv.at[l, 0], sibling)

    def stage_b(l):
        pc[l].wait_recv()
        mine = p_own[l, pl.ds(pl.multiple_of(half * core, half), half), :] + p_recv[l].astype(F32)
        x_slots[l, coord[0]] = mine.astype(BF16)
        xc[l] = [
            remote(x_slots.at[l, coord[0]], x_slots.at[l, coord[0]], x_send.at[l, k - 1], x_recv.at[l, k - 1], along(0, k))
            for k in (1, 2, 3)
        ]

    def stage_c(l):
        for c in xc[l]:
            c.wait_recv()
        total = x_slots[l, 0].astype(F32)
        for j in (1, 2, 3):
            total = total + x_slots[l, j].astype(F32)
        s_full[l, core] = total.astype(BF16)
        sc[l] = remote(s_full.at[l, core], s_full.at[l, core], core_send.at[l, 1], core_recv.at[l, 1], sibling)

    def stage_d(l):
        sc[l].wait_recv()
        for h in range(2):
            s_t[l, :, half * h:half * h + half] = s_full[l, h].T
        other = s_t[l, pl.ds(pl.multiple_of(R * (1 - core), R), R), :]
        w = jnp.dot(other, merged[l, 1 - core], preferred_element_type=F32)
        for j in range(4):
            w_send[l, j] = w[:, 256 * j:256 * j + 256].astype(BF16)
        wc[l] = remote(w_send.at[l], w_recv.at[l], core_send.at[l, 2], core_recv.at[l, 2], sibling)
        mine = s_t[l, pl.ds(pl.multiple_of(R * core, R), R), :]
        w = jnp.dot(mine, merged[l, core], preferred_element_type=F32)
        for j in range(4):
            w_own[l, j] = w[:, 256 * j:256 * j + 256]

    def spread(l, phase, axis, source, target):
        return [
            remote(source((coord[axis] + k) % 4), target(k), ax_send.at[l, phase, k - 1], ax_recv.at[l, phase, k - 1], along(axis, k))
            for k in (1, 2, 3)
        ]

    ac = {}

    def axes(l):
        return l % 3, (l + 1) % 3, (l + 2) % 3

    def stage_e(l):
        wc[l].wait_recv()
        w_sum[l] = (w_own[l] + w_recv[l].astype(F32)).astype(BF16)
        ac[l, 0] = spread(l, 0, axes(l)[0], lambda j: w_sum.at[l, j], lambda k: r1.at[l, k - 1])

    def row16(j):
        return pl.ds(pl.multiple_of(j * 16, 16), 16)

    def stage_f(l):
        for c in ac[l, 0]:
            c.wait_recv()
        total = w_sum[l, coord[axes(l)[0]]].astype(F32)
        for k in range(3):
            total = total + r1[l, k].astype(F32)
        s1[l] = total.astype(BF16)
        ac[l, 1] = spread(l, 1, axes(l)[1], lambda j: s1.at[l, row16(j)], lambda k: r2.at[l, k - 1])

    def stage_h(l):
        for c in ac[l, 1]:
            c.wait_recv()
        total = s1[l, row16(coord[axes(l)[1]]), :].astype(F32)
        for k in range(3):
            total = total + r2[l, k].astype(F32)
        mine = coord[axes(l)[2]]
        e_slots[l, mine] = total.astype(BF16)
        ac[l, 2] = spread(l, 2, axes(l)[2], lambda j: e_slots.at[l, mine], lambda k: e_slots.at[l, mine])

    def stage_i(l):
        for c in ac[l, 2]:
            c.wait_recv()
        total = e_slots[l, 0].astype(F32)
        for j in (1, 2, 3):
            total = total + e_slots[l, j].astype(F32)
        a0, a1 = coord[axes(l)[0]], coord[axes(l)[1]]
        w_all[l, core, a0, row16(a1), :] = total.astype(BF16)
        piece = w_all.at[l, core, a0, row16(a1)]
        ac[l, 3] = spread(l, 3, axes(l)[1], lambda j: piece, lambda k: piece)

    def stage_j(l):
        for c in ac[l, 3]:
            c.wait_recv()
        piece = w_all.at[l, core, coord[axes(l)[0]]]
        ac[l, 4] = spread(l, 4, axes(l)[0], lambda j: piece, lambda k: piece)

    def stage_k(l):
        for c in ac[l, 4]:
            c.wait_recv()
        ac[l, 5] = remote(w_all.at[l, core], w_all.at[l, core], core_send.at[l, 3], core_recv.at[l, 3], sibling)

    gc = {}

    def gram_a():
        grams = []
        for l in range(LAYERS):
            mine = s_t[l, pl.ds(pl.multiple_of(R * core, R), R), :]
            grams.append(lax.dot_general(mine, mine, NT, preferred_element_type=F32))
        slot = coord[1]
        gram_y[slot, 0:64, :] = jnp.concatenate([grams[0], grams[1]], axis=1)
        gram_y[slot, 64:96, :] = jnp.concatenate([grams[2][0:32], grams[2][32:64]], axis=1)
        gc[0] = [
            remote(gram_y.at[slot], gram_y.at[slot], gram_send.at[0, k - 1], gram_recv.at[0, k - 1], along(1, k)) for k in (1, 2, 3)
        ]

    def gram_b():
        for c in gc[0]:
            c.wait_recv()
        slot = coord[2]
        gram_z[slot] = ((gram_y[0] + gram_y[1]) + gram_y[2]) + gram_y[3]
        gc[1] = [
            remote(gram_z.at[slot], gram_z.at[slot], gram_send.at[1, k - 1], gram_recv.at[1, k - 1], along(2, k)) for k in (1, 2, 3)
        ]

    def gram_c():
        for c in gc[1]:
            c.wait_recv()
        total = ((gram_z[0] + gram_z[1]) + gram_z[2]) + gram_z[3]
        lane = lax.broadcasted_iota(jnp.int32, (R, 2 * R), 1)
        row = lax.broadcasted_iota(jnp.int32, (R, 2 * R), 0)
        eye = (lane == row + R).astype(F32)
        both, last = total[0:64], total[64:96]
        aug[0] = jnp.where(lane < R, both, eye)
        aug[1] = jnp.where(lane < R, pltpu.roll(both, R, 1), eye)
        aug[2] = jnp.where(lane < R, jnp.concatenate([last, pltpu.roll(last, R, 1)], axis=0), eye)

        def step(b, carry):
            for i in range(8):
                j = b * 8 + i
                for l in range(LAYERS):
                    pivot_row = aug[l, pl.ds(j, 1), :]
                    scaled = pivot_row / pivot_row[:, i:i + 1]
                    a = aug[l]
                    aug[l] = a - jnp.where(row > j, a[:, i:i + 1], 0.0) * scaled
            for l in range(LAYERS):
                aug[l] = pltpu.roll(aug[l], 2 * R - 8, 1)
            return carry

        lax.fori_loop(0, R // 8, step, 0)
        for l in range(LAYERS):
            a = aug[l]
            pivots = jnp.sum(jnp.where(lane == row + R, a, 0.0), axis=1, keepdims=True)
            linv[l, core] = jnp.where(lane < R, a * lax.rsqrt(pivots), 0.0)
        gc[2] = [
            remote(linv.at[l, core], linv.at[l, core], core_send.at[l, 4], core_recv.at[l, 4], sibling) for l in range(LAYERS)
        ]

    def gram_d():
        for l in range(LAYERS):
            gc[2][l].wait_recv()
        for l in range(LAYERS):
            block = jnp.concatenate([linv[l, 0], pltpu.roll(linv[l, 1], R, 1)], axis=0)
            high = block.astype(BF16)
            low = (block - high.astype(F32)).astype(BF16)
            for h in range(2):
                s = s_full[l, h]
                out = lax.dot_general(s, high, NT, preferred_element_type=F32)
                out = out + lax.dot_general(s, low, NT, preferred_element_type=F32)
                basis[l, half * h:half * h + half, :] = out.astype(BF16)

    stage_a(0)
    stage_a(1)
    stage_b(0)
    stage_a(2)
    stage_b(1)
    stage_b(2)
    stage_c(0)
    stage_c(1)
    stage_d(0)
    stage_c(2)
    stage_d(1)
    stage_e(0)
    stage_d(2)
    stage_e(1)
    stage_e(2)
    gram_a()
    for l in range(LAYERS):
        stage_f(l)
    gram_b()
    for l in range(LAYERS):
        stage_h(l)
    gram_c()
    for l in range(LAYERS):
        stage_i(l)
    gram_d()
    for l in range(LAYERS):
        stage_j(l)
    for l in range(LAYERS):
        stage_k(l)
    for l in range(LAYERS):
        ac[l, 5].wait_recv()
    for c in sends:
        c.wait_send()


def rebuild_kernel(replicas, merged, basis, w_all, linv, memory_out, rebuilt_out, query_out, qpad):
    m = pl.program_id(1)
    block = pl.program_id(2)

    @pl.when(block == 0)
    def _():
        inverse = linv[0, 0][:, 0:R]
        high = inverse.astype(BF16)
        low = (inverse - high.astype(F32)).astype(BF16)
        qpad[pl.ds(pl.multiple_of(R - R * m, R), R), :] = jnp.zeros((R, KVW), BF16)
        for j in range(4):
            w = w_all[0, 0, j]
            q = jnp.dot(high, w, preferred_element_type=F32) + jnp.dot(low, w, preferred_element_type=F32)
            q = q * (1.0 / replicas)
            query_out[0, 0, :, 256 * j:256 * j + 256] = q
            qpad[pl.ds(pl.multiple_of(R * m, R), R), 256 * j:256 * j + 256] = q.astype(BF16)

    rebuilt = jnp.dot(basis[0], qpad[...], preferred_element_type=F32)
    rebuilt_out[0, 0] = rebuilt.astype(BF16)
    memory_out[0, 0, 0] = (merged[0, 0].astype(F32) - rebuilt).astype(BF16)


def body(gradients, memory, initial_query):
    replicas = lax.axis_size("dp")
    vmem = pl.BlockSpec(memory_space=pltpu.VMEM)
    hbm = pl.BlockSpec(memory_space=pl.ANY)
    query_t = jnp.swapaxes(initial_query, 2, 3)
    half = ROWS // 2
    dma = pltpu.SemaphoreType.DMA
    merged, basis, w_all, linv = pl.pallas_call(
        reduce_kernel,
        name="reduce",
        out_shape=[
            pltpu.VMEM((LAYERS, 2, ROWS, KVW), BF16),
            pltpu.VMEM((LAYERS, ROWS, 2 * R), BF16),
            pltpu.VMEM((LAYERS, 2, 4, R, 256), BF16),
            pltpu.VMEM((LAYERS, 2, R, 2 * R), F32),
        ],
        in_specs=[hbm, hbm, vmem],
        out_specs=[vmem] * 4,
        scratch_shapes=[
            pltpu.VMEM((LAYERS, 2, ROWS, KVW), BF16),
            pltpu.VMEM((LAYERS, 2, ROWS, KVW), BF16),
            pltpu.VMEM((LAYERS, 2, 2 * R, KVW), BF16),
            pltpu.VMEM((LAYERS, ROWS, 2 * R), F32),
            pltpu.VMEM((LAYERS, half, 2 * R), BF16),
            pltpu.VMEM((LAYERS, half, 2 * R), BF16),
            pltpu.VMEM((LAYERS, 4, half, 2 * R), BF16),
            pltpu.VMEM((LAYERS, 2, half, 2 * R), BF16),
            pltpu.VMEM((LAYERS, 2 * R, ROWS), BF16),
            pltpu.VMEM((LAYERS, 4, R, 256), F32),
            pltpu.VMEM((LAYERS, 4, R, 256), BF16),
            pltpu.VMEM((LAYERS, 4, R, 256), BF16),
            pltpu.VMEM((LAYERS, 4, R, 256), BF16),
            pltpu.VMEM((LAYERS, 3, R, 256), BF16),
            pltpu.VMEM((LAYERS, R, 256), BF16),
            pltpu.VMEM((LAYERS, 3, 16, 256), BF16),
            pltpu.VMEM((LAYERS, 4, 16, 256), BF16),
            pltpu.VMEM((4, 96, 2 * R), F32),
            pltpu.VMEM((4, 96, 2 * R), F32),
            pltpu.VMEM((LAYERS, R, 2 * R), F32),
            pltpu.VMEM((8, 128), F32),
            dma((LAYERS, 2, 2)),
            dma((LAYERS, 5)),
            dma((LAYERS, 5)),
            dma((LAYERS, 3)),
            dma((LAYERS, 3)),
            dma((LAYERS, 5, 3)),
            dma((LAYERS, 5, 3)),
            dma((2, 3)),
            dma((2, 3)),
        ],
        compiler_params=pltpu.CompilerParams(collective_id=0, has_side_effects=True, vmem_limit_bytes=40 << 20),
    )(gradients, memory, query_t)

    blocks = 2
    rows = ROWS // blocks
    new_memory, rebuilt, query = pl.pallas_call(
        functools.partial(rebuild_kernel, replicas),
        name="rebuild",
        grid=(LAYERS, 2, blocks),
        out_shape=[
            jax.ShapeDtypeStruct((1, LAYERS, 2, ROWS, KVW), BF16),
            jax.ShapeDtypeStruct((LAYERS, 2, ROWS, KVW), BF16),
            jax.ShapeDtypeStruct((LAYERS, 2, R, KVW), F32),
        ],
        in_specs=[
            pl.BlockSpec((1, 1, rows, KVW), lambda l, m, b: (l, m, b, 0)),
            pl.BlockSpec((1, rows, 2 * R), lambda l, m, b: (l, b, 0)),
            pl.BlockSpec((1, 1, 4, R, 256), lambda l, m, b: (l, m, 0, 0, 0)),
            pl.BlockSpec((1, 1, R, 2 * R), lambda l, m, b: (l, m, 0, 0)),
        ],
        out_specs=[
            pl.BlockSpec((1, 1, 1, rows, KVW), lambda l, m, b: (0, l, m, b, 0)),
            pl.BlockSpec((1, 1, rows, KVW), lambda l, m, b: (l, m, b, 0)),
            pl.BlockSpec((1, 1, R, KVW), lambda l, m, b: (l, m, 0, 0)),
        ],
        scratch_shapes=[pltpu.VMEM((2 * R, KVW), BF16)],
        compiler_params=pltpu.CompilerParams(vmem_limit_bytes=20 << 20),
    )(merged, basis, w_all, linv)
    return new_memory, rebuilt, jnp.swapaxes(query, 2, 3)


def solution(mesh):
    in_specs = (P("dp", None, None, "tensor", None), P("dp", None, None, "tensor", None), P())
    out_specs = (P("dp", None, None, "tensor", None), P(None, None, "tensor", None), P())
    return jax.shard_map(body, mesh=mesh, in_specs=in_specs, out_specs=out_specs, check_vma=False)
```

time: 409 us -> 73.8 us (0.18)
  waiting for transfers between devices: 297 us -> 0 us
  Pallas kernels: 0 us -> 71.6 us
  other arithmetic: 67.5 us -> 0 us
  matrix products: 29.7 us -> 0 us
  between operations: 13.8 us -> 0.65 us
    psum x3 -> x0, waiting for transfers between devices: 297 us -> none  [the longest x1 149 us: body(): query_whole = lax.psum(projected, ('dp', 'tensor'))]
    pallas_call x0 -> x2, Pallas kernels: none -> 71.6 us  [the longest x1 62.3 us: body(): pl.pallas_call(reduce_kernel, name='reduce', out_shape=[pltpu.VMEM((LAYER...]
    another operation x7 -> x0, other arithmetic: 65 us -> none  [the longest x4 35.4 us: orthonormal_basis(): factor = jnp.linalg.cholesky(gram_product)]
    dot_general x4 -> x0, matrix products: 27.8 us -> none  [the longest x1 9.36 us: body(): jnp.einsum('lmdr,lmkr->lmdk', basis, query_next_low, preferred_element_ty...]
  transfers between devices with their start and end apart: 3 -> 0, of which waited for: 3 -> 0; matrix products, arithmetic and copies ran while one was open for 0% -> 0% of each run, Pallas kernels for 0% -> 0%
where the time goes in v1:
time: 73.8 us; the launch traced here: 73.6 us
  Pallas kernels  71.6 us (97%)
  local copies, waits for them, and re-layouts  1.4 us (2%)
    pallas_call x1, Pallas kernels, body(): pl.pallas_call(reduce_kernel, name='reduce', out_shape=[pltpu.VMEM((LAYER...  62.3 us
    pallas_call x1, Pallas kernels, body(): pl.pallas_call(functools.partial(rebuild_kernel, replicas), name='rebuild...  9.25 us

profile of v1, /device:TPU:1, one launch (start us, length us, event | category | flops | bytes accessed | tf_op | source)
XLA Modules:
  0.0 73.6 jit_solution(7213270316239122269)
XLA Ops:
  0.6 0.0 copy-start
  0.6 1.4 %copy-done = f32[3,2,1024,64]{2,3,1,0:T(8,128)S(1)} copy-done((f32[3,2,1024,64]{2,3,1,0:T(8,128)S(1)}, f32[3,2,1024,64]{2,3,1,0:T(8,128)}, u32[]{:S(2)}) %copy-start) | copy-done | bytes 1572888
  2.0 62.3 %reduce.1 = (bf16[3,2,512,1024]{3,2,1,0:T(8,128)(2,1)S(1)}, bf16[3,512,128]{2,1,0:T(8,128)(2,1)S(1)}, bf16[3,2,4,64,256]{4,3,2,1,0:T(8,128)(2,1)S(1)}, f32[3,2,64,128]{3,2,1,0:T(8,128)S(1)}) custom-call(bf16[1,3,2,512,1024]{4,3,2,1,0:T(8,128)(2,1)} %g_hbm.1, bf16[1,3,2,512,1024]{4,3,2,1,0:T(8,128)(2,1)} %m_hbm.1, f32[3,2,64,1024]{3,2,1,0:T(8,128)S(1)} %bitcast.2), custom_call_target="tpu_custom_call" | custom-call | tf_op jit(solution)/shard_map/reduce/pallas_call | solution.py:310
  64.4 9.2 %rebuild.1 = (bf16[1,3,2,512,1024]{4,3,2,1,0:T(8,128)(2,1)}, bf16[3,2,512,1024]{3,2,1,0:T(8,128)(2,1)}, f32[3,2,64,1024]{3,2,1,0:T(8,128)}) custom-call(bf16[3,2,512,1024]{3,2,1,0:T(8,128)(2,1)S(1)} %get-tuple-element.10.merged, bf16[3,512,128]{2,1,0:T(8,128)(2,1)S(1)} %get-tuple-element.11.basis, bf16[3,2,4,64,256]{4,3,2,1,0:T(8,128)(2,1)S(1)} %get-tuple-element.12.w_all, ...), custom_call_target="tpu_custom_call" | custom-call | tf_op jit(solution)/shard_map/rebuild/pallas_call | solution.py:358
Async XLA Ops:
  0.6 1.4 %copy-start = (f32[3,2,1024,64]{2,3,1,0:T(8,128)S(1)}, f32[3,2,1024,64]{2,3,1,0:T(8,128)}, u32[]{:S(2)}) copy-start(f32[3,2,1024,64]{2,3,1,0:T(8,128)} %param.5) | copy-start | bytes 4718596

commit v2 on v1

--- a/solution.py
+++ b/solution.py
@@ -14,15 +14,16 @@
 ROWS = 512
 KVW = 1024
 R = 64
+CHUNK = 256
 NT = (((1,), (1,)), ((), ()))
 
 
 def reduce_kernel(
-    g_hbm, m_hbm, query_ref,
+    g_hbm, m_hbm, query_hbm,
     merged, basis, w_all, linv,
-    g_buf, m_buf, qpad, p_own, p_send, p_recv, x_slots, s_full, s_t,
-    w_own, w_send, w_recv, w_sum, r1, s1, r2, e_slots, gram_y, gram_z, aug, linv_mine,
-    load_sem, core_send, core_recv, x_send, x_recv, ax_send, ax_recv, gram_send, gram_recv,
+    g_buf, m_buf, query, qpad, p_own, p_send, p_recv, x_slots, s_full, s_t,
+    w_own, w_send, w_recv, w_sum, r1, s1, r2, e_slots, gram_y, gram_z,
+    load_sem, query_sem, core_send, core_recv, x_send, x_recv, ax_send, ax_recv, gram_send, gram_recv,
 ):
     dp = lax.axis_index("dp")
     tensor = lax.axis_index("tensor")
@@ -36,6 +37,8 @@
 
     sibling = (dp + 1 - 2 * core, tensor)
 
+    query_load = pltpu.make_async_copy(query_hbm, query, query_sem)
+    query_load.start()
     loads = []
     for l in range(LAYERS):
         for m in range(2):
@@ -51,10 +54,12 @@
         for k in (1, 2, 3):
             pl.semaphore_signal(barrier, inc=1, device_id=along(axis, k), device_id_type=MESH)
 
+    query_load.wait()
+    column = lax.broadcasted_iota(jnp.int32, (KVW, 2 * R), 1)
     for l in range(LAYERS):
+        pair = jnp.concatenate([query[l, 0], query[l, 1]], axis=0).astype(BF16).T
         for m in range(2):
-            qpad[l, m, R * m:R * m + R, :] = query_ref[l, m].astype(BF16)
-            qpad[l, m, R - R * m:2 * R - R * m, :] = jnp.zeros((R, KVW), BF16)
+            qpad[l, m] = jnp.where((column >= R * m) & (column < R * m + R), pair, jnp.zeros_like(pair))
 
     sends = []
 
@@ -68,15 +73,16 @@
     pc, xc, sc, wc = {}, {}, {}, {}
 
     def stage_a(l):
-        total = None
         for m in range(2):
             a, b = loads[2 * l + m]
             a.wait()
             b.wait()
-            merged[l, m] = (g_buf[l, m].astype(F32) + m_buf[l, m].astype(F32)).astype(BF16)
-            part = lax.dot_general(merged[l, m], qpad[l, m], NT, preferred_element_type=F32)
-            total = part if total is None else total + part
-        p_own[l] = total
+            for r in range(0, ROWS, CHUNK):
+                rows = slice(r, r + CHUNK)
+                block = g_buf[l, m, rows] + m_buf[l, m, rows]
+                merged[l, m, rows] = block
+                part = jnp.dot(block, qpad[l, m], preferred_element_type=F32)
+                p_own[l, rows] = part if m == 0 else p_own[l, rows] + part
         p_send[l] = p_own[l, pl.ds(pl.multiple_of(half * (1 - core), half), half), :].astype(BF16)
         if l == 0:
             pl.semaphore_wait(barrier, 10)
@@ -205,25 +211,26 @@
         row = lax.broadcasted_iota(jnp.int32, (R, 2 * R), 0)
         eye = (lane == row + R).astype(F32)
         both, last = total[0:64], total[64:96]
-        aug[0] = jnp.where(lane < R, both, eye)
-        aug[1] = jnp.where(lane < R, pltpu.roll(both, R, 1), eye)
-        aug[2] = jnp.where(lane < R, jnp.concatenate([last, pltpu.roll(last, R, 1)], axis=0), eye)
+        start = (
+            jnp.where(lane < R, both, eye),
+            jnp.where(lane < R, pltpu.roll(both, R, 1), eye),
+            jnp.where(lane < R, jnp.concatenate([last, pltpu.roll(last, R, 1)], axis=0), eye),
+        )
 
         def step(b, carry):
+            left = row < R - 8 * b
+            state = list(carry)
             for i in range(8):
-                j = b * 8 + i
+                below = left & (row > i)
                 for l in range(LAYERS):
-                    pivot_row = aug[l, pl.ds(j, 1), :]
-                    scaled = pivot_row / pivot_row[:, i:i + 1]
-                    a = aug[l]
-                    aug[l] = a - jnp.where(row > j, a[:, i:i + 1], 0.0) * scaled
-            for l in range(LAYERS):
-                aug[l] = pltpu.roll(aug[l], 2 * R - 8, 1)
-            return carry
-
-        lax.fori_loop(0, R // 8, step, 0)
+                    a = state[l]
+                    scaled = a[i:i + 1, :] / a[i:i + 1, i:i + 1]
+                    state[l] = a - jnp.where(below, a[:, i:i + 1], 0.0) * scaled
+            return tuple(pltpu.roll(jnp.concatenate([a[8:], a[:8]], axis=0), 2 * R - 8, 1) for a in state)
+
+        done = lax.fori_loop(0, R // 8, step, start)
         for l in range(LAYERS):
-            a = aug[l]
+            a = done[l]
             pivots = jnp.sum(jnp.where(lane == row + R, a, 0.0), axis=1, keepdims=True)
             linv[l, core] = jnp.where(lane < R, a * lax.rsqrt(pivots), 0.0)
         gc[2] = [
@@ -243,67 +250,60 @@
                 out = out + lax.dot_general(s, low, NT, preferred_element_type=F32)
                 basis[l, half * h:half * h + half, :] = out.astype(BF16)
 
-    stage_a(0)
-    stage_a(1)
-    stage_b(0)
-    stage_a(2)
-    stage_b(1)
-    stage_b(2)
-    stage_c(0)
-    stage_c(1)
-    stage_d(0)
-    stage_c(2)
-    stage_d(1)
-    stage_e(0)
-    stage_d(2)
-    stage_e(1)
-    stage_e(2)
-    gram_a()
-    for l in range(LAYERS):
-        stage_f(l)
-    gram_b()
-    for l in range(LAYERS):
-        stage_h(l)
-    gram_c()
-    for l in range(LAYERS):
-        stage_i(l)
-    gram_d()
-    for l in range(LAYERS):
-        stage_j(l)
-    for l in range(LAYERS):
-        stage_k(l)
+    plan = [
+        (stage_a, 0), (stage_a, 1), (stage_b, 0), (stage_a, 2), (stage_b, 1), (stage_b, 2),
+        (stage_c, 0), (stage_c, 1), (stage_d, 0), (stage_c, 2), (stage_d, 1), (stage_e, 0), (stage_d, 2), (stage_e, 1), (stage_e, 2),
+        (gram_a,), (stage_f, 0), (stage_f, 1), (stage_f, 2), (gram_b,), (stage_h, 0), (stage_h, 1), (stage_h, 2), (gram_c,),
+        (stage_i, 0), (stage_i, 1), (stage_i, 2), (gram_d,), (stage_j, 0), (stage_j, 1), (stage_j, 2),
+        (stage_k, 0), (stage_k, 1), (stage_k, 2),
+    ]
+    for stage in plan:
+        stage[0](*stage[1:])
     for l in range(LAYERS):
         ac[l, 5].wait_recv()
     for c in sends:
         c.wait_send()
 
 
-def rebuild_kernel(replicas, merged, basis, w_all, linv, memory_out, rebuilt_out, query_out, qpad):
-    m = pl.program_id(1)
-    block = pl.program_id(2)
-
-    @pl.when(block == 0)
-    def _():
-        inverse = linv[0, 0][:, 0:R]
-        high = inverse.astype(BF16)
-        low = (inverse - high.astype(F32)).astype(BF16)
-        qpad[pl.ds(pl.multiple_of(R - R * m, R), R), :] = jnp.zeros((R, KVW), BF16)
-        for j in range(4):
-            w = w_all[0, 0, j]
-            q = jnp.dot(high, w, preferred_element_type=F32) + jnp.dot(low, w, preferred_element_type=F32)
-            q = q * (1.0 / replicas)
-            query_out[0, 0, :, 256 * j:256 * j + 256] = q
-            qpad[pl.ds(pl.multiple_of(R * m, R), R), 256 * j:256 * j + 256] = q.astype(BF16)
-
-    rebuilt = jnp.dot(basis[0], qpad[...], preferred_element_type=F32)
-    rebuilt_out[0, 0] = rebuilt.astype(BF16)
-    memory_out[0, 0, 0] = (merged[0, 0].astype(F32) - rebuilt).astype(BF16)
+def rebuild_kernel(
+    replicas, merged, basis, w_all, linv, memory_out, rebuilt_out, query_out, qpad, memory_buf, rebuilt_buf, query_buf, sem, query_sem
+):
+    copies = []
+
+    def write(src, dst, s):
+        c = pltpu.make_async_copy(src, dst, s)
+        c.start()
+        copies.append(c)
+
+    for l in range(LAYERS):
+        for m in range(2):
+            inverse = linv[l, m][:, 0:R]
+            high = inverse.astype(BF16)
+            low = (inverse - high.astype(F32)).astype(BF16)
+            qpad[l, m, R - R * m:2 * R - R * m, :] = jnp.zeros((R, KVW), BF16)
+            for j in range(4):
+                w = w_all[l, m, j]
+                q = jnp.dot(high, w, preferred_element_type=F32) + jnp.dot(low, w, preferred_element_type=F32)
+                q = q * (1.0 / replicas)
+                query_buf[l, m, :, 256 * j:256 * j + 256] = q
+                qpad[l, m, R * m:R * m + R, 256 * j:256 * j + 256] = q.astype(BF16)
+            write(query_buf.at[l, m], query_out.at[l, m], query_sem.at[l, m])
+            for n, r in enumerate(range(0, ROWS, CHUNK)):
+                rows = slice(r, r + CHUNK)
+                at = pl.ds(r, CHUNK)
+                rebuilt = jnp.dot(basis[l, rows], qpad[l, m], preferred_element_type=F32)
+                rebuilt_buf[l, m, rows] = rebuilt.astype(BF16)
+                memory_buf[l, m, rows] = (merged[l, m, rows].astype(F32) - rebuilt).astype(BF16)
+                write(rebuilt_buf.at[l, m, at], rebuilt_out.at[l, m, at], sem.at[l, m, n, 0])
+                write(memory_buf.at[l, m, at], memory_out.at[0, l, m, at], sem.at[l, m, n, 1])
+    for c in copies:
+        c.wait()
 
 
 def body(gradients, memory, initial_query):
     replicas = lax.axis_size("dp")
     vmem = pl.BlockSpec(memory_space=pltpu.VMEM)
-    hbm = pl.BlockSpec(memory_space=pl.ANY)
+    hbm = pl.BlockSpec(memory_space=pltpu.HBM)
     query_t = jnp.swapaxes(initial_query, 2, 3)
     half = ROWS // 2
     dma = pltpu.SemaphoreType.DMA
@@ -316,12 +316,13 @@
             pltpu.VMEM((LAYERS, 2, 4, R, 256), BF16),
             pltpu.VMEM((LAYERS, 2, R, 2 * R), F32),
         ],
-        in_specs=[hbm, hbm, vmem],
+        in_specs=[hbm, hbm, hbm],
         out_specs=[vmem] * 4,
         scratch_shapes=[
             pltpu.VMEM((LAYERS, 2, ROWS, KVW), BF16),
             pltpu.VMEM((LAYERS, 2, ROWS, KVW), BF16),
-            pltpu.VMEM((LAYERS, 2, 2 * R, KVW), BF16),
+            pltpu.VMEM((LAYERS, 2, R, KVW), F32),
+            pltpu.VMEM((LAYERS, 2, KVW, 2 * R), BF16),
             pltpu.VMEM((LAYERS, ROWS, 2 * R), F32),
             pltpu.VMEM((LAYERS, half, 2 * R), BF16),
             pltpu.VMEM((LAYERS, half, 2 * R), BF16),
@@ -338,9 +339,8 @@
             pltpu.VMEM((LAYERS, 4, 16, 256), BF16),
             pltpu.VMEM((4, 96, 2 * R), F32),
             pltpu.VMEM((4, 96, 2 * R), F32),
-            pltpu.VMEM((LAYERS, R, 2 * R), F32),
-            pltpu.VMEM((8, 128), F32),
             dma((LAYERS, 2, 2)),
+            dma,
             dma((LAYERS, 5)),
             dma((LAYERS, 5)),
             dma((LAYERS, 3)),
@@ -350,33 +350,28 @@
             dma((2, 3)),
             dma((2, 3)),
         ],
-        compiler_params=pltpu.CompilerParams(collective_id=0, has_side_effects=True, vmem_limit_bytes=40 << 20),
+        compiler_params=pltpu.CompilerParams(collective_id=0, has_side_effects=True, vmem_limit_bytes=54 << 20),
     )(gradients, memory, query_t)
 
-    blocks = 2
-    rows = ROWS // blocks
     new_memory, rebuilt, query = pl.pallas_call(
         functools.partial(rebuild_kernel, replicas),
         name="rebuild",
-        grid=(LAYERS, 2, blocks),
         out_shape=[
             jax.ShapeDtypeStruct((1, LAYERS, 2, ROWS, KVW), BF16),
             jax.ShapeDtypeStruct((LAYERS, 2, ROWS, KVW), BF16),
             jax.ShapeDtypeStruct((LAYERS, 2, R, KVW), F32),
         ],
-        in_specs=[
-            pl.BlockSpec((1, 1, rows, KVW), lambda l, m, b: (l, m, b, 0)),
-            pl.BlockSpec((1, rows, 2 * R), lambda l, m, b: (l, b, 0)),
-            pl.BlockSpec((1, 1, 4, R, 256), lambda l, m, b: (l, m, 0, 0, 0)),
-            pl.BlockSpec((1, 1, R, 2 * R), lambda l, m, b: (l, m, 0, 0)),
+        in_specs=[vmem] * 4,
+        out_specs=[hbm] * 3,
+        scratch_shapes=[
+            pltpu.VMEM((LAYERS, 2, 2 * R, KVW), BF16),
+            pltpu.VMEM((LAYERS, 2, ROWS, KVW), BF16),
+            pltpu.VMEM((LAYERS, 2, ROWS, KVW), BF16),
+            pltpu.VMEM((LAYERS, 2, R, KVW), F32),
+            dma((LAYERS, 2, ROWS // CHUNK, 2)),
+            dma((LAYERS, 2)),
         ],
-        out_specs=[
-            pl.BlockSpec((1, 1, 1, rows, KVW), lambda l, m, b: (0, l, m, b, 0)),
-            pl.BlockSpec((1, 1, rows, KVW), lambda l, m, b: (l, m, b, 0)),
-            pl.BlockSpec((1, 1, R, KVW), lambda l, m, b: (l, m, 0, 0)),
-        ],
-        scratch_shapes=[pltpu.VMEM((2 * R, KVW), BF16)],
-        compiler_params=pltpu.CompilerParams(vmem_limit_bytes=20 << 20),
+        compiler_params=pltpu.CompilerParams(vmem_limit_bytes=36 << 20),
     )(merged, basis, w_all, linv)
     return new_memory, rebuilt, jnp.swapaxes(query, 2, 3)
 

time: 73.8 us -> 60.5 us (0.82)
  Pallas kernels: 71.6 us -> 59.7 us
  local copies, waits for them, and re-layouts: 1.4 us -> 0 us
    pallas_call x1, Pallas kernels: 62.3 us -> 54 us  [body(): pl.pallas_call(reduce_kernel, name='reduce', out_shape=[pltpu.VMEM((LAYER...]
    pallas_call x1, Pallas kernels: 9.25 us -> 5.73 us  [body(): pl.pallas_call(functools.partial(rebuild_kernel, replicas), name='rebuild...]
    unnamed x2 -> x0, local copies, waits for them, and re-layouts: 1.4 us -> none
where the time goes in v2:
time: 60.5 us; the launch traced here: 60.4 us
  Pallas kernels  59.7 us (99%)
  between operations  0.64 us (1%)
    pallas_call x1, Pallas kernels, body(): pl.pallas_call(reduce_kernel, name='reduce', out_shape=[pltpu.VMEM((LAYER...  54 us
    pallas_call x1, Pallas kernels, body(): pl.pallas_call(functools.partial(rebuild_kernel, replicas), name='rebuild...  5.73 us

profile of v2, /device:TPU:1, one launch (start us, length us, event | category | flops | bytes accessed | tf_op | source)
XLA Modules:
  0.0 60.4 jit_solution(16987202936034560519)
XLA Ops:
  0.6 54.0 %reduce.1 = (bf16[3,2,512,1024]{3,2,1,0:T(8,128)(2,1)S(1)}, bf16[3,512,128]{2,1,0:T(8,128)(2,1)S(1)}, bf16[3,2,4,64,256]{4,3,2,1,0:T(8,128)(2,1)S(1)}, f32[3,2,64,128]{3,2,1,0:T(8,128)S(1)}) custom-call(bf16[1,3,2,512,1024]{4,3,2,1,0:T(8,128)(2,1)} %g_hbm.1, bf16[1,3,2,512,1024]{4,3,2,1,0:T(8,128)(2,1)} %m_hbm.1, f32[3,2,64,1024]{3,2,1,0:T(8,128)} %bitcast.2), custom_call_target="tpu_custom_call" | custom-call | tf_op jit(solution)/shard_map/reduce/pallas_call | solution.py:310
  54.6 5.7 %rebuild.1 = (bf16[1,3,2,512,1024]{4,3,2,1,0:T(8,128)(2,1)}, bf16[3,2,512,1024]{3,2,1,0:T(8,128)(2,1)}, f32[3,2,64,1024]{3,2,1,0:T(8,128)}) custom-call(bf16[3,2,512,1024]{3,2,1,0:T(8,128)(2,1)S(1)} %get-tuple-element.10.merged, bf16[3,512,128]{2,1,0:T(8,128)(2,1)S(1)} %get-tuple-element.11.basis, bf16[3,2,4,64,256]{4,3,2,1,0:T(8,128)(2,1)S(1)} %get-tuple-element.12.w_all, ...), custom_call_target="tpu_custom_call" | custom-call | tf_op jit(solution)/shard_map/rebuild/pallas_call | solution.py:356

commit v3 on v2

--- a/solution.py
+++ b/solution.py
@@ -15,6 +15,7 @@
 KVW = 1024
 R = 64
 CHUNK = 256
+DEPTH = 3
 NT = (((1,), (1,)), ((), ()))
 
 
@@ -22,7 +23,7 @@
     g_hbm, m_hbm, query_hbm,
     merged, basis, w_all, linv,
     g_buf, m_buf, query, qpad, p_own, p_send, p_recv, x_slots, s_full, s_t,
-    w_own, w_send, w_recv, w_sum, r1, s1, r2, e_slots, gram_y, gram_z,
+    w_own, w_send, w_recv, w_sum, r1, e1, e2, gram_y, gram_z, aug,
     load_sem, query_sem, core_send, core_recv, x_send, x_recv, ax_send, ax_recv, gram_send, gram_recv,
 ):
     dp = lax.axis_index("dp")
@@ -37,16 +38,24 @@
 
     sibling = (dp + 1 - 2 * core, tensor)
 
-    query_load = pltpu.make_async_copy(query_hbm, query, query_sem)
-    query_load.start()
-    loads = []
-    for l in range(LAYERS):
-        for m in range(2):
-            a = pltpu.make_async_copy(g_hbm.at[0, l, m], g_buf.at[l, m], load_sem.at[l, m, 0])
-            b = pltpu.make_async_copy(m_hbm.at[0, l, m], m_buf.at[l, m], load_sem.at[l, m, 1])
-            a.start()
-            b.start()
-            loads.append((a, b))
+    query_loads = [pltpu.make_async_copy(query_hbm.at[l], query.at[l], query_sem.at[l]) for l in range(LAYERS)]
+    loads = [
+        (
+            pltpu.make_async_copy(g_hbm.at[0, l, m], g_buf.at[l, m], load_sem.at[l, m, 0]),
+            pltpu.make_async_copy(m_hbm.at[0, l, m], m_buf.at[l, m], load_sem.at[l, m, 1]),
+        )
+        for l in range(LAYERS)
+        for m in range(2)
+    ]
+
+    def load(i):
+        if i % 2 == 0:
+            query_loads[i // 2].start()
+        loads[i][0].start()
+        loads[i][1].start()
+
+    for i in range(DEPTH):
+        load(i)
 
     barrier = pltpu.get_barrier_semaphore()
     pl.semaphore_signal(barrier, inc=1, device_id=sibling, device_id_type=MESH)
@@ -54,9 +63,10 @@
         for k in (1, 2, 3):
             pl.semaphore_signal(barrier, inc=1, device_id=along(axis, k), device_id_type=MESH)
 
-    query_load.wait()
     column = lax.broadcasted_iota(jnp.int32, (KVW, 2 * R), 1)
-    for l in range(LAYERS):
+
+    def right_factor(l):
+        query_loads[l].wait()
         pair = jnp.concatenate([query[l, 0], query[l, 1]], axis=0).astype(BF16).T
         for m in range(2):
             qpad[l, m] = jnp.where((column >= R * m) & (column < R * m + R), pair, jnp.zeros_like(pair))
@@ -73,10 +83,13 @@
     pc, xc, sc, wc = {}, {}, {}, {}
 
     def stage_a(l):
+        right_factor(l)
         for m in range(2):
-            a, b = loads[2 * l + m]
-            a.wait()
-            b.wait()
+            i = 2 * l + m
+            loads[i][0].wait()
+            loads[i][1].wait()
+            if i + DEPTH < len(loads):
+                load(i + DEPTH)
             for r in range(0, ROWS, CHUNK):
                 rows = slice(r, r + CHUNK)
                 block = g_buf[l, m, rows] + m_buf[l, m, rows]
@@ -136,49 +149,42 @@
         w_sum[l] = (w_own[l] + w_recv[l].astype(F32)).astype(BF16)
         ac[l, 0] = spread(l, 0, axes(l)[0], lambda j: w_sum.at[l, j], lambda k: r1.at[l, k - 1])
 
-    def row16(j):
-        return pl.ds(pl.multiple_of(j * 16, 16), 16)
-
     def stage_f(l):
         for c in ac[l, 0]:
             c.wait_recv()
         total = w_sum[l, coord[axes(l)[0]]].astype(F32)
         for k in range(3):
             total = total + r1[l, k].astype(F32)
-        s1[l] = total.astype(BF16)
-        ac[l, 1] = spread(l, 1, axes(l)[1], lambda j: s1.at[l, row16(j)], lambda k: r2.at[l, k - 1])
+        mine = coord[axes(l)[1]]
+        e1[l, mine] = total.astype(BF16)
+        ac[l, 1] = spread(l, 1, axes(l)[1], lambda j: e1.at[l, mine], lambda k: e1.at[l, mine])
+
+    def in_order(slots):
+        return ((slots[0].astype(F32) + slots[1].astype(F32)) + slots[2].astype(F32)) + slots[3].astype(F32)
 
     def stage_h(l):
         for c in ac[l, 1]:
             c.wait_recv()
-        total = s1[l, row16(coord[axes(l)[1]]), :].astype(F32)
-        for k in range(3):
-            total = total + r2[l, k].astype(F32)
         mine = coord[axes(l)[2]]
-        e_slots[l, mine] = total.astype(BF16)
-        ac[l, 2] = spread(l, 2, axes(l)[2], lambda j: e_slots.at[l, mine], lambda k: e_slots.at[l, mine])
+        e2[l, mine] = in_order(e1.at[l]).astype(BF16)
+        ac[l, 2] = spread(l, 2, axes(l)[2], lambda j: e2.at[l, mine], lambda k: e2.at[l, mine])
+
+    def forward(l, j, k):
+        piece = w_all.at[l, core, j]
+        ac[l, 4, k] = remote(piece, piece, core_send.at[l, 4 + k], core_recv.at[l, 4 + k], sibling)
 
     def stage_i(l):
         for c in ac[l, 2]:
             c.wait_recv()
-        total = e_slots[l, 0].astype(F32)
-        for j in (1, 2, 3):
-            total = total + e_slots[l, j].astype(F32)
-        a0, a1 = coord[axes(l)[0]], coord[axes(l)[1]]
-        w_all[l, core, a0, row16(a1), :] = total.astype(BF16)
-        piece = w_all.at[l, core, a0, row16(a1)]
-        ac[l, 3] = spread(l, 3, axes(l)[1], lambda j: piece, lambda k: piece)
-
-    def stage_j(l):
-        for c in ac[l, 3]:
-            c.wait_recv()
-        piece = w_all.at[l, core, coord[axes(l)[0]]]
-        ac[l, 4] = spread(l, 4, axes(l)[0], lambda j: piece, lambda k: piece)
-
-    def stage_k(l):
-        for c in ac[l, 4]:
-            c.wait_recv()
-        ac[l, 5] = remote(w_all.at[l, core], w_all.at[l, core], core_send.at[l, 3], core_recv.at[l, 3], sibling)
+        mine = coord[axes(l)[0]]
+        w_all[l, core, mine] = in_order(e2.at[l]).astype(BF16)
+        piece = w_all.at[l, core, mine]
+        ac[l, 3] = spread(l, 3, axes(l)[0], lambda j: piece, lambda k: piece)
+        forward(l, mine, 0)
+
+    def stage_k(l, k):
+        ac[l, 3][k - 1].wait_recv()
+        forward(l, (coord[axes(l)[0]] + 4 - k) % 4, k)
 
     gc = {}
 
@@ -211,11 +217,12 @@
         row = lax.broadcasted_iota(jnp.int32, (R, 2 * R), 0)
         eye = (lane == row + R).astype(F32)
         both, last = total[0:64], total[64:96]
-        start = (
-            jnp.where(lane < R, both, eye),
-            jnp.where(lane < R, pltpu.roll(both, R, 1), eye),
-            jnp.where(lane < R, jnp.concatenate([last, pltpu.roll(last, R, 1)], axis=0), eye),
-        )
+        aug[0] = jnp.where(lane < R, both, eye)
+        aug[1] = jnp.where(lane < R, pltpu.roll(both, R, 1), eye)
+        aug[2] = jnp.where(lane < R, jnp.concatenate([last, pltpu.roll(last, R, 1)], axis=0), eye)
+
+    def eliminate(first, end):
+        row = lax.broadcasted_iota(jnp.int32, (R, 2 * R), 0)
 
         def step(b, carry):
             left = row < R - 8 * b
@@ -228,13 +235,19 @@
                     state[l] = a - jnp.where(below, a[:, i:i + 1], 0.0) * scaled
             return tuple(pltpu.roll(jnp.concatenate([a[8:], a[:8]], axis=0), 2 * R - 8, 1) for a in state)
 
-        done = lax.fori_loop(0, R // 8, step, start)
-        for l in range(LAYERS):
-            a = done[l]
+        done = lax.fori_loop(first, end, step, tuple(aug[l] for l in range(LAYERS)))
+        for l in range(LAYERS):
+            aug[l] = done[l]
+
+    def invert():
+        lane = lax.broadcasted_iota(jnp.int32, (R, 2 * R), 1)
+        row = lax.broadcasted_iota(jnp.int32, (R, 2 * R), 0)
+        for l in range(LAYERS):
+            a = aug[l]
             pivots = jnp.sum(jnp.where(lane == row + R, a, 0.0), axis=1, keepdims=True)
             linv[l, core] = jnp.where(lane < R, a * lax.rsqrt(pivots), 0.0)
         gc[2] = [
-            remote(linv.at[l, core], linv.at[l, core], core_send.at[l, 4], core_recv.at[l, 4], sibling) for l in range(LAYERS)
+            remote(linv.at[l, core], linv.at[l, core], core_send.at[l, 3], core_recv.at[l, 3], sibling) for l in range(LAYERS)
         ]
 
     def gram_d():
@@ -253,14 +266,16 @@
     plan = [
         (stage_a, 0), (stage_a, 1), (stage_b, 0), (stage_a, 2), (stage_b, 1), (stage_b, 2),
         (stage_c, 0), (stage_c, 1), (stage_d, 0), (stage_c, 2), (stage_d, 1), (stage_e, 0), (stage_d, 2), (stage_e, 1), (stage_e, 2),
-        (gram_a,), (stage_f, 0), (stage_f, 1), (stage_f, 2), (gram_b,), (stage_h, 0), (stage_h, 1), (stage_h, 2), (gram_c,),
-        (stage_i, 0), (stage_i, 1), (stage_i, 2), (gram_d,), (stage_j, 0), (stage_j, 1), (stage_j, 2),
-        (stage_k, 0), (stage_k, 1), (stage_k, 2),
+        (gram_a,), (stage_f, 0), (stage_f, 1), (stage_f, 2), (gram_b,), (stage_h, 0), (stage_h, 1), (stage_h, 2),
+        (gram_c,), (eliminate, 0, 4), (stage_i, 0), (stage_i, 1), (stage_i, 2), (eliminate, 4, 8), (invert,),
+        (stage_k, 0, 1), (stage_k, 1, 1), (stage_k, 2, 1), (stage_k, 0, 3), (stage_k, 1, 3), (stage_k, 2, 3),
+        (stage_k, 0, 2), (stage_k, 1, 2), (stage_k, 2, 2), (gram_d,),
     ]
     for stage in plan:
         stage[0](*stage[1:])
     for l in range(LAYERS):
-        ac[l, 5].wait_recv()
+        for k in range(4):
+            ac[l, 4, k].wait_recv()
     for c in sends:
         c.wait_send()
 
@@ -334,19 +349,19 @@
             pltpu.VMEM((LAYERS, 4, R, 256), BF16),
             pltpu.VMEM((LAYERS, 4, R, 256), BF16),
             pltpu.VMEM((LAYERS, 3, R, 256), BF16),
-            pltpu.VMEM((LAYERS, R, 256), BF16),
-            pltpu.VMEM((LAYERS, 3, 16, 256), BF16),
-            pltpu.VMEM((LAYERS, 4, 16, 256), BF16),
+            pltpu.VMEM((LAYERS, 4, R, 256), BF16),
+            pltpu.VMEM((LAYERS, 4, R, 256), BF16),
             pltpu.VMEM((4, 96, 2 * R), F32),
             pltpu.VMEM((4, 96, 2 * R), F32),
+            pltpu.VMEM((LAYERS, R, 2 * R), F32),
             dma((LAYERS, 2, 2)),
-            dma,
-            dma((LAYERS, 5)),
-            dma((LAYERS, 5)),
+            dma((LAYERS,)),
+            dma((LAYERS, 8)),
+            dma((LAYERS, 8)),
             dma((LAYERS, 3)),
             dma((LAYERS, 3)),
-            dma((LAYERS, 5, 3)),
-            dma((LAYERS, 5, 3)),
+            dma((LAYERS, 4, 3)),
+            dma((LAYERS, 4, 3)),
             dma((2, 3)),
             dma((2, 3)),
         ],

time: 60.5 us -> 51.2 us (0.85)
  Pallas kernels: 59.7 us -> 50.4 us
    pallas_call x1, Pallas kernels: 54 us -> 44.7 us  [body(): pl.pallas_call(reduce_kernel, name='reduce', out_shape=[pltpu.VMEM((LAYER...]
where the time goes in v3:
time: 51.2 us; the launch traced here: 51.1 us
  Pallas kernels  50.4 us (98%)
  between operations  0.64 us (1%)
    pallas_call x1, Pallas kernels, body(): pl.pallas_call(reduce_kernel, name='reduce', out_shape=[pltpu.VMEM((LAYER...  44.7 us
    pallas_call x1, Pallas kernels, body(): pl.pallas_call(functools.partial(rebuild_kernel, replicas), name='rebuild...  5.72 us

profile of v3, /device:TPU:1, one launch (start us, length us, event | category | flops | bytes accessed | tf_op | source)
XLA Modules:
  0.0 51.1 jit_solution(1726482352936857403)
XLA Ops:
  0.6 44.7 %reduce.1 = (bf16[3,2,512,1024]{3,2,1,0:T(8,128)(2,1)S(1)}, bf16[3,512,128]{2,1,0:T(8,128)(2,1)S(1)}, bf16[3,2,4,64,256]{4,3,2,1,0:T(8,128)(2,1)S(1)}, f32[3,2,64,128]{3,2,1,0:T(8,128)S(1)}) custom-call(bf16[1,3,2,512,1024]{4,3,2,1,0:T(8,128)(2,1)} %g_hbm.1, bf16[1,3,2,512,1024]{4,3,2,1,0:T(8,128)(2,1)} %m_hbm.1, f32[3,2,64,1024]{3,2,1,0:T(8,128)} %bitcast.2), custom_call_target="tpu_custom_call" | custom-call | tf_op jit(solution)/shard_map/reduce/pallas_call | solution.py:325
  45.4 5.7 %rebuild.1 = (bf16[1,3,2,512,1024]{4,3,2,1,0:T(8,128)(2,1)}, bf16[3,2,512,1024]{3,2,1,0:T(8,128)(2,1)}, f32[3,2,64,1024]{3,2,1,0:T(8,128)}) custom-call(bf16[3,2,512,1024]{3,2,1,0:T(8,128)(2,1)S(1)} %get-tuple-element.10.merged, bf16[3,512,128]{2,1,0:T(8,128)(2,1)S(1)} %get-tuple-element.11.basis, bf16[3,2,4,64,256]{4,3,2,1,0:T(8,128)(2,1)S(1)} %get-tuple-element.12.w_all, ...), custom_call_target="tpu_custom_call" | custom-call | tf_op jit(solution)/shard_map/rebuild/pallas_call | solution.py:371

commit v4 on v3

--- a/solution.py
+++ b/solution.py
@@ -22,7 +22,7 @@
 def reduce_kernel(
     g_hbm, m_hbm, query_hbm,
     merged, basis, w_all, linv,
-    g_buf, m_buf, query, qpad, p_own, p_send, p_recv, x_slots, s_full, s_t,
+    g_buf, m_buf, query, qpad, p_own, p_send, p_recv, x_own, x_part, s_full, s_t,
     w_own, w_send, w_recv, w_sum, r1, e1, e2, gram_y, gram_z, aug,
     load_sem, query_sem, core_send, core_recv, x_send, x_recv, ax_send, ax_recv, gram_send, gram_recv,
 ):
@@ -101,22 +101,33 @@
             pl.semaphore_wait(barrier, 10)
         pc[l] = remote(p_send.at[l], p_recv.at[l], core_send.at[l, 0], core_recv.at[l, 0], sibling)
 
+    def row64(j):
+        return pl.ds(pl.multiple_of(j * 64, 64), 64)
+
     def stage_b(l):
         pc[l].wait_recv()
         mine = p_own[l, pl.ds(pl.multiple_of(half * core, half), half), :] + p_recv[l].astype(F32)
-        x_slots[l, coord[0]] = mine.astype(BF16)
+        x = coord[0]
+        x_own[l] = mine.astype(BF16)
         xc[l] = [
-            remote(x_slots.at[l, coord[0]], x_slots.at[l, coord[0]], x_send.at[l, k - 1], x_recv.at[l, k - 1], along(0, k))
+            remote(x_own.at[l, row64((x + k) % 4)], x_part.at[l, k - 1], x_send.at[l, 0, k - 1], x_recv.at[l, 0, k - 1], along(0, k))
             for k in (1, 2, 3)
         ]
 
+    def stage_r(l):
+        for c in xc[l]:
+            c.wait_recv()
+        x = coord[0]
+        total = x_own[l, row64(x), :].astype(F32)
+        for k in range(3):
+            total = total + x_part[l, k].astype(F32)
+        piece = s_full.at[l, core, row64(x)]
+        s_full[l, core, row64(x), :] = total.astype(BF16)
+        xc[l] = [remote(piece, piece, x_send.at[l, 1, k - 1], x_recv.at[l, 1, k - 1], along(0, k)) for k in (1, 2, 3)]
+
     def stage_c(l):
         for c in xc[l]:
             c.wait_recv()
-        total = x_slots[l, 0].astype(F32)
-        for j in (1, 2, 3):
-            total = total + x_slots[l, j].astype(F32)
-        s_full[l, core] = total.astype(BF16)
         sc[l] = remote(s_full.at[l, core], s_full.at[l, core], core_send.at[l, 1], core_recv.at[l, 1], sibling)
 
     def stage_d(l):
@@ -265,6 +276,7 @@
 
     plan = [
         (stage_a, 0), (stage_a, 1), (stage_b, 0), (stage_a, 2), (stage_b, 1), (stage_b, 2),
+        (stage_r, 0), (stage_r, 1), (stage_r, 2),
         (stage_c, 0), (stage_c, 1), (stage_d, 0), (stage_c, 2), (stage_d, 1), (stage_e, 0), (stage_d, 2), (stage_e, 1), (stage_e, 2),
         (gram_a,), (stage_f, 0), (stage_f, 1), (stage_f, 2), (gram_b,), (stage_h, 0), (stage_h, 1), (stage_h, 2),
         (gram_c,), (eliminate, 0, 4), (stage_i, 0), (stage_i, 1), (stage_i, 2), (eliminate, 4, 8), (invert,),
@@ -341,7 +353,8 @@
             pltpu.VMEM((LAYERS, ROWS, 2 * R), F32),
             pltpu.VMEM((LAYERS, half, 2 * R), BF16),
             pltpu.VMEM((LAYERS, half, 2 * R), BF16),
-            pltpu.VMEM((LAYERS, 4, half, 2 * R), BF16),
+            pltpu.VMEM((LAYERS, half, 2 * R), BF16),
+            pltpu.VMEM((LAYERS, 3, 64, 2 * R), BF16),
             pltpu.VMEM((LAYERS, 2, half, 2 * R), BF16),
             pltpu.VMEM((LAYERS, 2 * R, ROWS), BF16),
             pltpu.VMEM((LAYERS, 4, R, 256), F32),
@@ -358,8 +371,8 @@
             dma((LAYERS,)),
             dma((LAYERS, 8)),
             dma((LAYERS, 8)),
-            dma((LAYERS, 3)),
-            dma((LAYERS, 3)),
+            dma((LAYERS, 2, 3)),
+            dma((LAYERS, 2, 3)),
             dma((LAYERS, 4, 3)),
             dma((LAYERS, 4, 3)),
             dma((2, 3)),

time: 51.2 us -> 50.3 us (0.982)
  Pallas kernels: 50.4 us -> 49.5 us
    pallas_call x1, Pallas kernels: 44.7 us -> 43.8 us  [body(): pl.pallas_call(reduce_kernel, name='reduce', out_shape=[pltpu.VMEM((LAYER...]
where the time goes in v4:
time: 50.3 us; the launch traced here: 50.1 us
  Pallas kernels  49.5 us (98%)
  between operations  0.64 us (1%)
    pallas_call x1, Pallas kernels, body(): pl.pallas_call(reduce_kernel, name='reduce', out_shape=[pltpu.VMEM((LAYER...  43.8 us
    pallas_call x1, Pallas kernels, body(): pl.pallas_call(functools.partial(rebuild_kernel, replicas), name='rebuild...  5.73 us

profile of v4, /device:TPU:1, one launch (start us, length us, event | category | flops | bytes accessed | tf_op | source)
XLA Modules:
  0.0 50.1 jit_solution(11260604951937641348)
XLA Ops:
  0.6 43.8 %reduce.1 = (bf16[3,2,512,1024]{3,2,1,0:T(8,128)(2,1)S(1)}, bf16[3,512,128]{2,1,0:T(8,128)(2,1)S(1)}, bf16[3,2,4,64,256]{4,3,2,1,0:T(8,128)(2,1)S(1)}, f32[3,2,64,128]{3,2,1,0:T(8,128)S(1)}) custom-call(bf16[1,3,2,512,1024]{4,3,2,1,0:T(8,128)(2,1)} %g_hbm.1, bf16[1,3,2,512,1024]{4,3,2,1,0:T(8,128)(2,1)} %m_hbm.1, f32[3,2,64,1024]{3,2,1,0:T(8,128)} %bitcast.2), custom_call_target="tpu_custom_call" | custom-call | tf_op jit(solution)/shard_map/reduce/pallas_call | solution.py:337
  44.4 5.7 %rebuild.1 = (bf16[1,3,2,512,1024]{4,3,2,1,0:T(8,128)(2,1)}, bf16[3,2,512,1024]{3,2,1,0:T(8,128)(2,1)}, f32[3,2,64,1024]{3,2,1,0:T(8,128)}) custom-call(bf16[3,2,512,1024]{3,2,1,0:T(8,128)(2,1)S(1)} %get-tuple-element.10.merged, bf16[3,512,128]{2,1,0:T(8,128)(2,1)S(1)} %get-tuple-element.11.basis, bf16[3,2,4,64,256]{4,3,2,1,0:T(8,128)(2,1)S(1)} %get-tuple-element.12.w_all, ...), custom_call_target="tpu_custom_call" | custom-call | tf_op jit(solution)/shard_map/rebuild/pallas_call | solution.py:384

commit v5 on v4

v5 whole, which is shorter than its diff:
```python
import functools

import jax
import jax.numpy as jnp
from jax import lax
from jax.experimental import pallas as pl
from jax.experimental.pallas import tpu as pltpu
from jax.sharding import PartitionSpec as P

MESH = pl.DeviceIdType.MESH
F32 = jnp.float32
BF16 = jnp.bfloat16
LAYERS = 3
ROWS = 512
KVW = 1024
R = 64
CHUNK = 256
DEPTH = 4
NT = (((1,), (1,)), ((), ()))


def reduce_kernel(
    g_hbm, m_hbm, query_hbm,
    merged, basis, w_all, linv,
    g_buf, m_buf, query, qpad, p_own, p_send, p_recv, x_own, x_part, s_full, s_t,
    w_own, w_send, w_recv, w_sum, r1, e1, e2, gram_y, gram_z, aug,
    load_sem, query_sem, send, core_recv, x_recv, w_arrive, gram_recv, end_recv,
):
    dp = lax.axis_index("dp")
    tensor = lax.axis_index("tensor")
    core = dp % 2
    coord = (dp // 2, tensor // 4, tensor % 4)

    def along(axis, k):
        c = [coord[0], coord[1], coord[2]]
        c[axis] = (c[axis] + k) % 4
        return (c[0] * 2 + core, c[1] * 4 + c[2])

    sibling = (dp + 1 - 2 * core, tensor)

    query_loads = [pltpu.make_async_copy(query_hbm.at[l], query.at[l], query_sem.at[l]) for l in range(LAYERS)]
    loads = [
        (
            pltpu.make_async_copy(g_hbm.at[0, l, m], g_buf.at[l, m], load_sem.at[l, m]),
            pltpu.make_async_copy(m_hbm.at[0, l, m], m_buf.at[l, m], load_sem.at[l, m]),
        )
        for l in range(LAYERS)
        for m in range(2)
    ]

    def load(i):
        if i % 2 == 0:
            query_loads[i // 2].start()
        loads[i][0].start()
        loads[i][1].start()

    for i in range(DEPTH):
        load(i)

    barrier = pltpu.get_barrier_semaphore()
    pl.semaphore_signal(barrier, inc=1, device_id=sibling, device_id_type=MESH)
    for axis in range(3):
        for k in (1, 2, 3):
            pl.semaphore_signal(barrier, inc=1, device_id=along(axis, k), device_id_type=MESH)

    column = lax.broadcasted_iota(jnp.int32, (KVW, 2 * R), 1)

    def right_factor(l):
        query_loads[l].wait()
        pair = jnp.concatenate([query[l, 0], query[l, 1]], axis=0).astype(BF16).T
        for m in range(2):
            qpad[l, m] = jnp.where((column >= R * m) & (column < R * m + R), pair, jnp.zeros_like(pair))

    def remote(src, dst, send_sem, recv_sem, device):
        c = pltpu.make_async_remote_copy(src, dst, send_sem, recv_sem, device_id=device, device_id_type=MESH)
        c.start()
        return c

    def drain(like, sem):
        pltpu.make_async_copy(like, like, sem).wait()

    half = ROWS // 2

    def stage_a(l):
        right_factor(l)
        for m in range(2):
            i = 2 * l + m
            drain(g_buf.at[0], load_sem.at[l, m])
            if i + DEPTH < len(loads):
                load(i + DEPTH)
            for r in range(0, ROWS, CHUNK):
                rows = slice(r, r + CHUNK)
                block = g_buf[l, m, rows] + m_buf[l, m, rows]
                merged[l, m, rows] = block
                part = jnp.dot(block, qpad[l, m], preferred_element_type=F32)
                p_own[l, rows] = part if m == 0 else p_own[l, rows] + part
        p_send[l] = p_own[l, pl.ds(pl.multiple_of(half * (1 - core), half), half), :].astype(BF16)
        if l == 0:
            pl.semaphore_wait(barrier, 10)
        remote(p_send.at[l], p_recv.at[l], send.at[0], core_recv.at[l, 0], sibling)

    def row64(j):
        return pl.ds(pl.multiple_of(j * 64, 64), 64)

    def stage_b(l):
        drain(p_recv.at[l], core_recv.at[l, 0])
        mine = p_own[l, pl.ds(pl.multiple_of(half * core, half), half), :] + p_recv[l].astype(F32)
        x = coord[0]
        x_own[l] = mine.astype(BF16)
        for k in (1, 2, 3):
            remote(x_own.at[l, row64((x + k) % 4)], x_part.at[l, k - 1], send.at[1], x_recv.at[l, 0], along(0, k))

    def stage_r(l):
        drain(x_part.at[l], x_recv.at[l, 0])
        x = coord[0]
        total = x_own[l, row64(x), :].astype(F32)
        for k in range(3):
            total = total + x_part[l, k].astype(F32)
        piece = s_full.at[l, core, row64(x)]
        s_full[l, core, row64(x), :] = total.astype(BF16)
        for k in (1, 2, 3):
            remote(piece, piece, send.at[2], x_recv.at[l, 1], along(0, k))

    def stage_c(l):
        drain(x_part.at[l], x_recv.at[l, 1])
        remote(s_full.at[l, core], s_full.at[l, core], send.at[3], core_recv.at[l, 1], sibling)

    def stage_d(l):
        drain(p_recv.at[l], core_recv.at[l, 1])
        for h in range(2):
            s_t[l, :, half * h:half * h + half] = s_full[l, h].T
        other = s_t[l, pl.ds(pl.multiple_of(R * (1 - core), R), R), :]
        w = jnp.dot(other, merged[l, 1 - core], preferred_element_type=F32)
        for j in range(4):
            w_send[l, j] = w[:, 256 * j:256 * j + 256].astype(BF16)
        remote(w_send.at[l], w_recv.at[l], send.at[4], core_recv.at[l, 2], sibling)
        mine = s_t[l, pl.ds(pl.multiple_of(R * core, R), R), :]
        w = jnp.dot(mine, merged[l, core], preferred_element_type=F32)
        for j in range(4):
            w_own[l, j] = w[:, 256 * j:256 * j + 256]

    def axes(l, h):
        return (l + h) % 3, (l + h + 1) % 3, (l + h + 2) % 3

    def stage_e(l):
        drain(w_recv.at[l], core_recv.at[l, 2])
        w_sum[l] = (w_own[l] + w_recv[l].astype(F32)).astype(BF16)
        for h in range(2):
            axis = axes(l, h)[0]
            for k in (1, 2, 3):
                piece = w_sum.at[l, (coord[axis] + k) % 4, pl.ds(32 * h, 32)]
                remote(piece, r1.at[l, h, k - 1], send.at[5], w_arrive.at[l, h, 0], along(axis, k))

    def exchange(slots, l, h, phase, value):
        axis = axes(l, h)[phase]
        piece = slots.at[l, h, coord[axis]]
        slots[l, h, coord[axis]] = value.astype(BF16)
        for k in (1, 2, 3):
            remote(piece, piece, send.at[5 + phase], w_arrive.at[l, h, phase], along(axis, k))

    def stage_f(l):
        for h in range(2):
            drain(r1.at[l, h], w_arrive.at[l, h, 0])
            total = w_sum[l, coord[axes(l, h)[0]], 32 * h:32 * h + 32, :].astype(F32)
            for k in range(3):
                total = total + r1[l, h, k].astype(F32)
            exchange(e1, l, h, 1, total)

    def in_order(slots):
        return ((slots[0].astype(F32) + slots[1].astype(F32)) + slots[2].astype(F32)) + slots[3].astype(F32)

    def stage_h(l):
        for h in range(2):
            drain(r1.at[l, h], w_arrive.at[l, h, 1])
            exchange(e2, l, h, 2, in_order(e1.at[l, h]))

    def forward(l, h, j):
        piece = w_all.at[l, core, j, pl.ds(32 * h, 32)]
        remote(piece, piece, send.at[9], end_recv.at[0], sibling)

    def stage_i(l):
        for h in range(2):
            drain(r1.at[l, h], w_arrive.at[l, h, 2])
            axis = axes(l, h)[0]
            mine = coord[axis]
            w_all[l, core, mine, 32 * h:32 * h + 32, :] = in_order(e2.at[l, h]).astype(BF16)
            piece = w_all.at[l, core, mine, pl.ds(32 * h, 32)]
            for k in (1, 2, 3):
                remote(piece, piece, send.at[8], w_arrive.at[l, h, 2 + k], along(axis, k))
            forward(l, h, mine)

    def stage_k(l, k):
        for h in range(2):
            drain(r1.at[l, h, 0], w_arrive.at[l, h, 2 + k])
            forward(l, h, (coord[axes(l, h)[0]] + 4 - k) % 4)

    def gram(l):
        mine = s_t[l, pl.ds(pl.multiple_of(R * core, R), R), :]
        return lax.dot_general(mine, mine, NT, preferred_element_type=F32)

    def gram_a(first, rows):
        slot = coord[1]
        if first == 0:
            gram_y[slot, 0:64, :] = jnp.concatenate([gram(0), gram(1)], axis=1)
        else:
            last = gram(2)
            gram_y[slot, 64:96, :] = jnp.concatenate([last[0:32], last[32:64]], axis=1)
        piece = gram_y.at[slot, pl.ds(first, rows)]
        for k in (1, 2, 3):
            remote(piece, piece, send.at[10], gram_recv.at[first // 64], along(1, k))

    def gram_b():
        drain(gram_y.at[pl.ds(0, 3), pl.ds(0, 64)], gram_recv.at[0])
        drain(gram_y.at[pl.ds(0, 3), pl.ds(64, 32)], gram_recv.at[1])
        slot = coord[2]
        gram_z[slot] = ((gram_y[0] + gram_y[1]) + gram_y[2]) + gram_y[3]
        for k in (1, 2, 3):
            remote(gram_z.at[slot], gram_z.at[slot], send.at[11], gram_recv.at[2], along(2, k))

    def gram_c():
        drain(gram_z.at[pl.ds(0, 3)], gram_recv.at[2])
        total = ((gram_z[0] + gram_z[1]) + gram_z[2]) + gram_z[3]
        lane = lax.broadcasted_iota(jnp.int32, (R, 2 * R), 1)
        row = lax.broadcasted_iota(jnp.int32, (R, 2 * R), 0)
        eye = (lane == row + R).astype(F32)
        both, last = total[0:64], total[64:96]
        aug[0] = jnp.where(lane < R, both, eye)
        aug[1] = jnp.where(lane < R, pltpu.roll(both, R, 1), eye)
        aug[2] = jnp.where(lane < R, jnp.concatenate([last, pltpu.roll(last, R, 1)], axis=0), eye)

    def eliminate(first, end):
        row = lax.broadcasted_iota(jnp.int32, (R, 2 * R), 0)

        def step(b, carry):
            left = row < R - 8 * b
            state = list(carry)
            for i in range(8):
                below = left & (row > i)
                for l in range(LAYERS):
                    a = state[l]
                    scaled = a[i:i + 1, :] / a[i:i + 1, i:i + 1]
                    state[l] = a - jnp.where(below, a[:, i:i + 1], 0.0) * scaled
            return tuple(pltpu.roll(jnp.concatenate([a[8:], a[:8]], axis=0), 2 * R - 8, 1) for a in state)

        done = lax.fori_loop(first, end, step, tuple(aug[l] for l in range(LAYERS)))
        for l in range(LAYERS):
            aug[l] = done[l]

    def invert():
        lane = lax.broadcasted_iota(jnp.int32, (R, 2 * R), 1)
        row = lax.broadcasted_iota(jnp.int32, (R, 2 * R), 0)
        for l in range(LAYERS):
            a = aug[l]
            pivots = jnp.sum(jnp.where(lane == row + R, a, 0.0), axis=1, keepdims=True)
            linv[l, core] = jnp.where(lane < R, a * lax.rsqrt(pivots), 0.0)
            remote(linv.at[l, core], linv.at[l, core], send.at[12], end_recv.at[1], sibling)

    def gram_d():
        drain(aug, end_recv.at[1])
        for l in range(LAYERS):
            block = jnp.concatenate([linv[l, 0], pltpu.roll(linv[l, 1], R, 1)], axis=0)
            high = block.astype(BF16)
            low = (block - high.astype(F32)).astype(BF16)
            for h in range(2):
                s = s_full[l, h]
                out = lax.dot_general(s, high, NT, preferred_element_type=F32)
                out = out + lax.dot_general(s, low, NT, preferred_element_type=F32)
                basis[l, half * h:half * h + half, :] = out.astype(BF16)

    plan = [
        (stage_a, 0), (stage_a, 1), (stage_b, 0), (stage_a, 2), (stage_b, 1), (stage_b, 2),
        (stage_r, 0), (stage_r, 1), (stage_r, 2),
        (stage_c, 0), (stage_c, 1), (stage_d, 0), (stage_c, 2), (stage_d, 1), (stage_e, 0), (stage_d, 2), (stage_e, 1),
        (gram_a, 0, 64), (stage_e, 2), (gram_a, 64, 32),
        (stage_f, 0), (stage_f, 1), (stage_f, 2), (gram_b,), (stage_h, 0), (stage_h, 1), (stage_h, 2),
        (gram_c,), (eliminate, 0, 4), (stage_i, 0), (stage_i, 1), (stage_i, 2), (eliminate, 4, 8), (invert,),
        (stage_k, 0, 1), (stage_k, 0, 3), (stage_k, 0, 2), (stage_k, 1, 1), (stage_k, 1, 3), (stage_k, 1, 2),
        (stage_k, 2, 1), (stage_k, 2, 3), (stage_k, 2, 2), (gram_d,),
    ]
    for stage in plan:
        stage[0](*stage[1:])
    drain(w_recv, end_recv.at[0])
    for n, like in enumerate(
        (p_recv, x_part, x_part, p_recv, w_recv, r1, r1, r1, r1, w_recv, gram_y.at[pl.ds(0, 3)], gram_z.at[pl.ds(0, 3)], aug)
    ):
        drain(like, send.at[n])


def rebuild_kernel(
    replicas, merged, basis, w_all, linv, memory_out, rebuilt_out, query_out, qpad, memory_buf, rebuilt_buf, query_buf, sem
):
    def write(src, dst, n):
        pltpu.make_async_copy(src, dst, sem.at[n]).start()

    for l in range(LAYERS):
        for m in range(2):
            inverse = linv[l, m][:, 0:R]
            high = inverse.astype(BF16)
            low = (inverse - high.astype(F32)).astype(BF16)
            qpad[l, m, R - R * m:2 * R - R * m, :] = jnp.zeros((R, KVW), BF16)
            for j in range(4):
                w = w_all[l, m, j]
                q = jnp.dot(high, w, preferred_element_type=F32) + jnp.dot(low, w, preferred_element_type=F32)
                q = q * (1.0 / replicas)
                query_buf[l, m, :, 256 * j:256 * j + 256] = q
                qpad[l, m, R * m:R * m + R, 256 * j:256 * j + 256] = q.astype(BF16)
            write(query_buf.at[l, m], query_out.at[l, m], 0)
            for r in range(0, ROWS, CHUNK):
                rows = slice(r, r + CHUNK)
                at = pl.ds(r, CHUNK)
                rebuilt = jnp.dot(basis[l, rows], qpad[l, m], preferred_element_type=F32)
                rebuilt_buf[l, m, rows] = rebuilt.astype(BF16)
                memory_buf[l, m, rows] = (merged[l, m, rows].astype(F32) - rebuilt).astype(BF16)
                write(rebuilt_buf.at[l, m, at], rebuilt_out.at[l, m, at], 1)
                write(memory_buf.at[l, m, at], memory_out.at[0, l, m, at], 2)
    for n, buffer in enumerate((query_buf, rebuilt_buf, memory_buf)):
        pltpu.make_async_copy(buffer, buffer, sem.at[n]).wait()


def body(gradients, memory, initial_query):
    replicas = lax.axis_size("dp")
    vmem = pl.BlockSpec(memory_space=pltpu.VMEM)
    hbm = pl.BlockSpec(memory_space=pltpu.HBM)
    query_t = jnp.swapaxes(initial_query, 2, 3)
    half = ROWS // 2
    dma = pltpu.SemaphoreType.DMA
    merged, basis, w_all, linv = pl.pallas_call(
        reduce_kernel,
        name="reduce",
        out_shape=[
            pltpu.VMEM((LAYERS, 2, ROWS, KVW), BF16),
            pltpu.VMEM((LAYERS, ROWS, 2 * R), BF16),
            pltpu.VMEM((LAYERS, 2, 4, R, 256), BF16),
            pltpu.VMEM((LAYERS, 2, R, 2 * R), F32),
        ],
        in_specs=[hbm, hbm, hbm],
        out_specs=[vmem] * 4,
        scratch_shapes=[
            pltpu.VMEM((LAYERS, 2, ROWS, KVW), BF16),
            pltpu.VMEM((LAYERS, 2, ROWS, KVW), BF16),
            pltpu.VMEM((LAYERS, 2, R, KVW), F32),
            pltpu.VMEM((LAYERS, 2, KVW, 2 * R), BF16),
            pltpu.VMEM((LAYERS, ROWS, 2 * R), F32),
            pltpu.VMEM((LAYERS, half, 2 * R), BF16),
            pltpu.VMEM((LAYERS, half, 2 * R), BF16),
            pltpu.VMEM((LAYERS, half, 2 * R), BF16),
            pltpu.VMEM((LAYERS, 3, 64, 2 * R), BF16),
            pltpu.VMEM((LAYERS, 2, half, 2 * R), BF16),
            pltpu.VMEM((LAYERS, 2 * R, ROWS), BF16),
            pltpu.VMEM((LAYERS, 4, R, 256), F32),
            pltpu.VMEM((LAYERS, 4, R, 256), BF16),
            pltpu.VMEM((LAYERS, 4, R, 256), BF16),
            pltpu.VMEM((LAYERS, 4, R, 256), BF16),
            pltpu.VMEM((LAYERS, 2, 3, 32, 256), BF16),
            pltpu.VMEM((LAYERS, 2, 4, 32, 256), BF16),
            pltpu.VMEM((LAYERS, 2, 4, 32, 256), BF16),
            pltpu.VMEM((4, 96, 2 * R), F32),
            pltpu.VMEM((4, 96, 2 * R), F32),
            pltpu.VMEM((LAYERS, R, 2 * R), F32),
            dma((LAYERS, 2)),
            dma((LAYERS,)),
            dma((13,)),
            dma((LAYERS, 3)),
            dma((LAYERS, 2)),
            dma((LAYERS, 2, 6)),
            dma((3,)),
            dma((2,)),
        ],
        compiler_params=pltpu.CompilerParams(collective_id=0, has_side_effects=True, vmem_limit_bytes=54 << 20),
    )(gradients, memory, query_t)

    new_memory, rebuilt, query = pl.pallas_call(
        functools.partial(rebuild_kernel, replicas),
        name="rebuild",
        out_shape=[
            jax.ShapeDtypeStruct((1, LAYERS, 2, ROWS, KVW), BF16),
            jax.ShapeDtypeStruct((LAYERS, 2, ROWS, KVW), BF16),
            jax.ShapeDtypeStruct((LAYERS, 2, R, KVW), F32),
        ],
        in_specs=[vmem] * 4,
        out_specs=[hbm] * 3,
        scratch_shapes=[
            pltpu.VMEM((LAYERS, 2, 2 * R, KVW), BF16),
            pltpu.VMEM((LAYERS, 2, ROWS, KVW), BF16),
            pltpu.VMEM((LAYERS, 2, ROWS, KVW), BF16),
            pltpu.VMEM((LAYERS, 2, R, KVW), F32),
            dma((3,)),
        ],
        compiler_params=pltpu.CompilerParams(vmem_limit_bytes=36 << 20),
    )(merged, basis, w_all, linv)
    return new_memory, rebuilt, jnp.swapaxes(query, 2, 3)


def solution(mesh):
    in_specs = (P("dp", None, None, "tensor", None), P("dp", None, None, "tensor", None), P())
    out_specs = (P("dp", None, None, "tensor", None), P(None, None, "tensor", None), P())
    return jax.shard_map(body, mesh=mesh, in_specs=in_specs, out_specs=out_specs, check_vma=False)
```

time: 50.3 us -> 48.3 us (0.960)
  Pallas kernels: 49.5 us -> 47.6 us
    pallas_call x1, Pallas kernels: 43.8 us -> 42.2 us  [body(): pl.pallas_call(reduce_kernel, name='reduce', out_shape=[pltpu.VMEM((LAYER...]
where the time goes in v5:
time: 48.3 us; the launch traced here: 48.2 us
  Pallas kernels  47.6 us (99%)
  between operations  0.64 us (1%)
    pallas_call x1, Pallas kernels, body(): pl.pallas_call(reduce_kernel, name='reduce', out_shape=[pltpu.VMEM((LAYER...  42.2 us
    pallas_call x1, Pallas kernels, body(): pl.pallas_call(functools.partial(rebuild_kernel, replicas), name='rebuild...  5.4 us

profile of v5, /device:TPU:1, one launch (start us, length us, event | category | flops | bytes accessed | tf_op | source)
XLA Modules:
  0.0 48.2 jit_solution(3820548268084723347)
XLA Ops:
  0.6 42.2 %reduce.1 = (bf16[3,2,512,1024]{3,2,1,0:T(8,128)(2,1)S(1)}, bf16[3,512,128]{2,1,0:T(8,128)(2,1)S(1)}, bf16[3,2,4,64,256]{4,3,2,1,0:T(8,128)(2,1)S(1)}, f32[3,2,64,128]{3,2,1,0:T(8,128)S(1)}) custom-call(bf16[1,3,2,512,1024]{4,3,2,1,0:T(8,128)(2,1)} %g_hbm.1, bf16[1,3,2,512,1024]{4,3,2,1,0:T(8,128)(2,1)} %m_hbm.1, f32[3,2,64,1024]{3,2,1,0:T(8,128)} %bitcast.2), custom_call_target="tpu_custom_call" | custom-call | tf_op jit(solution)/shard_map/reduce/pallas_call | solution.py:327
  42.8 5.4 %rebuild.1 = (bf16[1,3,2,512,1024]{4,3,2,1,0:T(8,128)(2,1)}, bf16[3,2,512,1024]{3,2,1,0:T(8,128)(2,1)}, f32[3,2,64,1024]{3,2,1,0:T(8,128)}) custom-call(bf16[3,2,512,1024]{3,2,1,0:T(8,128)(2,1)S(1)} %get-tuple-element.10.merged, bf16[3,512,128]{2,1,0:T(8,128)(2,1)S(1)} %get-tuple-element.11.basis, bf16[3,2,4,64,256]{4,3,2,1,0:T(8,128)(2,1)S(1)} %get-tuple-element.12.w_all, ...), custom_call_target="tpu_custom_call" | custom-call | tf_op jit(solution)/shard_map/rebuild/pallas_call | solution.py:372

commit v6 on v5

v6 whole, which is shorter than its diff:
```python
import functools

import jax
import jax.numpy as jnp
from jax import lax
from jax.experimental import pallas as pl
from jax.experimental.pallas import tpu as pltpu
from jax.sharding import PartitionSpec as P

MESH = pl.DeviceIdType.MESH
F32 = jnp.float32
BF16 = jnp.bfloat16
LAYERS = 3
ROWS = 512
KVW = 1024
R = 64
CHUNK = 256
DEPTH = 4
NT = (((1,), (1,)), ((), ()))


def reduce_kernel(
    g_hbm, m_hbm, query_hbm,
    merged, basis, w_all, linv,
    g_buf, m_buf, query, qpad, p_own, p_send, p_part, s_full, s_t, w_send, r1, e1, e2, gram_y, gram_z, aug,
    load_sem, query_sem, send, s_recv, w_arrive, gram_recv, linv_recv,
):
    dp = lax.axis_index("dp")
    tensor = lax.axis_index("tensor")
    core = dp % 2
    coord = (dp // 2, tensor // 4, tensor % 4)

    def along(axis, k, other=0):
        c = [coord[0], coord[1], coord[2]]
        c[axis] = (c[axis] + k) % 4
        return (c[0] * 2 + (core + other) % 2, c[1] * 4 + c[2])

    sibling = (dp + 1 - 2 * core, tensor)

    query_loads = [pltpu.make_async_copy(query_hbm.at[l], query.at[l], query_sem.at[l]) for l in range(LAYERS)]
    loads = [
        (
            pltpu.make_async_copy(g_hbm.at[0, l, m], g_buf.at[l, m], load_sem.at[l, m]),
            pltpu.make_async_copy(m_hbm.at[0, l, m], m_buf.at[l, m], load_sem.at[l, m]),
        )
        for l in range(LAYERS)
        for m in range(2)
    ]

    def load(i):
        if i % 2 == 0:
            query_loads[i // 2].start()
        loads[i][0].start()
        loads[i][1].start()

    for i in range(DEPTH):
        load(i)

    barrier = pltpu.get_barrier_semaphore()
    pl.semaphore_signal(barrier, inc=1, device_id=sibling, device_id_type=MESH)
    for axis in range(3):
        for k in (1, 2, 3):
            for other in range(2):
                pl.semaphore_signal(barrier, inc=1, device_id=along(axis, k, other), device_id_type=MESH)

    column = lax.broadcasted_iota(jnp.int32, (KVW, 2 * R), 1)

    def right_factor(l):
        query_loads[l].wait()
        pair = jnp.concatenate([query[l, 0], query[l, 1]], axis=0).astype(BF16).T
        for m in range(2):
            qpad[l, m] = jnp.where((column >= R * m) & (column < R * m + R), pair, jnp.zeros_like(pair))

    def remote(src, dst, send_sem, recv_sem, device):
        c = pltpu.make_async_remote_copy(src, dst, send_sem, recv_sem, device_id=device, device_id_type=MESH)
        c.start()
        return c

    def drain(like, sem):
        pltpu.make_async_copy(like, like, sem).wait()

    partners = [(k, other) for k in (2, 1, 3) for other in range(2)] + [(0, 1)]
    half = ROWS // 2

    def row64(j):
        return pl.ds(pl.multiple_of(j * 64, 64), 64)

    def stage_a(l):
        right_factor(l)
        for m in range(2):
            i = 2 * l + m
            drain(g_buf.at[0], load_sem.at[l, m])
            if i + DEPTH < len(loads):
                load(i + DEPTH)
            for r in range(0, ROWS, CHUNK):
                rows = slice(r, r + CHUNK)
                block = g_buf[l, m, rows] + m_buf[l, m, rows]
                merged[l, m, rows] = block
                part = jnp.dot(block, qpad[l, m], preferred_element_type=F32)
                p_own[l, rows] = part if m == 0 else p_own[l, rows] + part
        p_send[l] = p_own[l].astype(BF16)
        if l == 0:
            pl.semaphore_wait(barrier, 19)
        for n, (k, other) in enumerate(partners):
            owner = (coord[0] + k) % 4 * 2 + (core + other) % 2
            remote(p_send.at[l, row64(owner)], p_part.at[l, n], send.at[0], s_recv.at[l, 0], along(0, k, other))

    def stage_r(l):
        drain(p_part.at[l], s_recv.at[l, 0])
        total = p_send[l, row64(dp), :].astype(F32)
        for n in range(len(partners)):
            total = total + p_part[l, n].astype(F32)
        piece = s_full.at[l, row64(dp)]
        s_full[l, row64(dp), :] = total.astype(BF16)
        for k, other in partners:
            remote(piece, piece, send.at[1], s_recv.at[l, 1], along(0, k, other))

    def stage_d(l):
        drain(p_part.at[l], s_recv.at[l, 1])
        s_t[l] = s_full[l].T
        for m in range(2):
            w = jnp.dot(s_t[l, R * m:R * m + R, :], merged[l, m], preferred_element_type=F32)
            for j in range(4):
                w_send[l, m, j] = w[:, 256 * j:256 * j + 256].astype(BF16)
        for h in range(2):
            axis = axes(l, h)[0]
            for n, (k, other) in enumerate(partners):
                piece = w_send.at[l, (core + other) % 2, (coord[axis] + k) % 4, pl.ds(32 * h, 32)]
                remote(piece, r1.at[l, h, n], send.at[2], w_arrive.at[l, h, 0], along(axis, k, other))

    def axes(l, h):
        return (l + h) % 3, (l + h + 1) % 3, (l + h + 2) % 3

    def exchange(slots, l, h, phase, value):
        axis = axes(l, h)[phase]
        piece = slots.at[l, h, coord[axis]]
        slots[l, h, coord[axis]] = value.astype(BF16)
        for k in (1, 2, 3):
            remote(piece, piece, send.at[2 + phase], w_arrive.at[l, h, phase], along(axis, k))

    def stage_f(l):
        for h in range(2):
            drain(r1.at[l, h], w_arrive.at[l, h, 0])
            total = w_send[l, core, coord[axes(l, h)[0]], 32 * h:32 * h + 32, :].astype(F32)
            for n in range(len(partners)):
                total = total + r1[l, h, n].astype(F32)
            exchange(e1, l, h, 1, total)

    def in_order(slots):
        return ((slots[0].astype(F32) + slots[1].astype(F32)) + slots[2].astype(F32)) + slots[3].astype(F32)

    def stage_h(l):
        for h in range(2):
            drain(r1.at[l, h, pl.ds(0, 3)], w_arrive.at[l, h, 1])
            exchange(e2, l, h, 2, in_order(e1.at[l, h]))

    def stage_i(l):
        for h in range(2):
            drain(r1.at[l, h, pl.ds(0, 3)], w_arrive.at[l, h, 2])
            axis = axes(l, h)[0]
            mine = coord[axis]
            w_all[l, core, mine, 32 * h:32 * h + 32, :] = in_order(e2.at[l, h]).astype(BF16)
            piece = w_all.at[l, core, mine, pl.ds(32 * h, 32)]
            for k, other in partners:
                remote(piece, piece, send.at[5], w_arrive.at[l, h, 3], along(axis, k, other))

    def stage_k(l):
        for h in range(2):
            drain(r1.at[l, h], w_arrive.at[l, h, 3])

    def gram(l):
        mine = s_t[l, pl.ds(pl.multiple_of(R * core, R), R), :]
        return lax.dot_general(mine, mine, NT, preferred_element_type=F32)

    def gram_a(first, rows):
        slot = coord[1]
        if first == 0:
            gram_y[slot, 0:64, :] = jnp.concatenate([gram(0), gram(1)], axis=1)
        else:
            last = gram(2)
            gram_y[slot, 64:96, :] = jnp.concatenate([last[0:32], last[32:64]], axis=1)
        piece = gram_y.at[slot, pl.ds(first, rows)]
        for k in (1, 2, 3):
            remote(piece, piece, send.at[6], gram_recv.at[first // 64], along(1, k))

    def gram_b():
        drain(gram_y.at[pl.ds(0, 3), pl.ds(0, 64)], gram_recv.at[0])
        drain(gram_y.at[pl.ds(0, 3), pl.ds(64, 32)], gram_recv.at[1])
        slot = coord[2]
        gram_z[slot] = ((gram_y[0] + gram_y[1]) + gram_y[2]) + gram_y[3]
        for k in (1, 2, 3):
            remote(gram_z.at[slot], gram_z.at[slot], send.at[7], gram_recv.at[2], along(2, k))

    def gram_c():
        drain(gram_z.at[pl.ds(0, 3)], gram_recv.at[2])
        total = ((gram_z[0] + gram_z[1]) + gram_z[2]) + gram_z[3]
        lane = lax.broadcasted_iota(jnp.int32, (R, 2 * R), 1)
        row = lax.broadcasted_iota(jnp.int32, (R, 2 * R), 0)
        eye = (lane == row + R).astype(F32)
        both, last = total[0:64], total[64:96]
        aug[0] = jnp.where(lane < R, both, eye)
        aug[1] = jnp.where(lane < R, pltpu.roll(both, R, 1), eye)
        aug[2] = jnp.where(lane < R, jnp.concatenate([last, pltpu.roll(last, R, 1)], axis=0), eye)

    def eliminate(first, end):
        row = lax.broadcasted_iota(jnp.int32, (8, 2 * R), 0)
        state = [aug[l, 8 * first:R, :] for l in range(LAYERS)]
        for b in range(first, end):
            top = [a[0:8] for a in state]
            state = [a[8:] for a in state]
            for i in range(8):
                j = 8 * b + i
                for l in range(LAYERS):
                    scaled = top[l][i:i + 1, :] / top[l][i:i + 1, j:j + 1]
                    top[l] = top[l] - jnp.where(row > i, top[l][:, j:j + 1], 0.0) * scaled
                    if j < R - 8:
                        state[l] = state[l] - state[l][:, j:j + 1] * scaled
            for l in range(LAYERS):
                aug[l, 8 * b:8 * b + 8, :] = top[l]
        if end < R // 8:
            for l in range(LAYERS):
                aug[l, 8 * end:R, :] = state[l]

    def invert():
        lane = lax.broadcasted_iota(jnp.int32, (R, 2 * R), 1)
        row = lax.broadcasted_iota(jnp.int32, (R, 2 * R), 0)
        for l in range(LAYERS):
            a = aug[l]
            pivots = jnp.sum(jnp.where(lane == row, a, 0.0), axis=1, keepdims=True)
            linv[l, core] = jnp.where(lane < R, pltpu.roll(a, R, 1) * lax.rsqrt(pivots), 0.0)
            remote(linv.at[l, core], linv.at[l, core], send.at[8], linv_recv, sibling)

    def gram_d():
        drain(aug, linv_recv)
        for l in range(LAYERS):
            block = jnp.concatenate([linv[l, 0], pltpu.roll(linv[l, 1], R, 1)], axis=0)
            high = block.astype(BF16)
            low = (block - high.astype(F32)).astype(BF16)
            for h in range(2):
                s = s_full[l, half * h:half * h + half, :]
                out = lax.dot_general(s, high, NT, preferred_element_type=F32)
                out = out + lax.dot_general(s, low, NT, preferred_element_type=F32)
                basis[l, half * h:half * h + half, :] = out.astype(BF16)

    plan = [
        (stage_a, 0), (stage_a, 1), (stage_a, 2), (stage_r, 0), (stage_r, 1), (stage_r, 2),
        (stage_d, 0), (stage_d, 1), (gram_a, 0, 64), (stage_d, 2), (gram_a, 64, 32),
        (stage_f, 0), (stage_f, 1), (stage_f, 2), (gram_b,), (stage_h, 0), (stage_h, 1), (stage_h, 2),
        (gram_c,), (eliminate, 0, 5), (stage_i, 0), (stage_i, 1), (stage_i, 2), (eliminate, 5, 8), (invert,), (gram_d,),
        (stage_k, 0), (stage_k, 1), (stage_k, 2),
    ]
    for stage in plan:
        stage[0](*stage[1:])
    few = r1.at[pl.ds(0, LAYERS), pl.ds(0, 2), pl.ds(0, 3)]
    for n, like in enumerate((p_part, p_part, r1, few, few, r1, gram_y.at[pl.ds(0, 3)], gram_z.at[pl.ds(0, 3)], aug)):
        drain(like, send.at[n])


def rebuild_kernel(
    replicas, merged, basis, w_all, linv, memory_out, rebuilt_out, query_out, qpad, memory_buf, rebuilt_buf, query_buf, sem
):
    def write(src, dst, n):
        pltpu.make_async_copy(src, dst, sem.at[n]).start()

    for l in range(LAYERS):
        for m in range(2):
            inverse = linv[l, m][:, 0:R]
            high = inverse.astype(BF16)
            low = (inverse - high.astype(F32)).astype(BF16)
            qpad[l, m, R - R * m:2 * R - R * m, :] = jnp.zeros((R, KVW), BF16)
            for j in range(4):
                w = w_all[l, m, j]
                q = jnp.dot(high, w, preferred_element_type=F32) + jnp.dot(low, w, preferred_element_type=F32)
                q = q * (1.0 / replicas)
                query_buf[l, m, :, 256 * j:256 * j + 256] = q
                qpad[l, m, R * m:R * m + R, 256 * j:256 * j + 256] = q.astype(BF16)
            write(query_buf.at[l, m], query_out.at[l, m], 0)
            for r in range(0, ROWS, CHUNK):
                rows = slice(r, r + CHUNK)
                at = pl.ds(r, CHUNK)
                rebuilt = jnp.dot(basis[l, rows], qpad[l, m], preferred_element_type=F32)
                rebuilt_buf[l, m, rows] = rebuilt.astype(BF16)
                memory_buf[l, m, rows] = (merged[l, m, rows].astype(F32) - rebuilt).astype(BF16)
                write(rebuilt_buf.at[l, m, at], rebuilt_out.at[l, m, at], 1)
                write(memory_buf.at[l, m, at], memory_out.at[0, l, m, at], 2)
    for n, buffer in enumerate((query_buf, rebuilt_buf, memory_buf)):
        pltpu.make_async_copy(buffer, buffer, sem.at[n]).wait()


def body(gradients, memory, initial_query):
    replicas = lax.axis_size("dp")
    vmem = pl.BlockSpec(memory_space=pltpu.VMEM)
    hbm = pl.BlockSpec(memory_space=pltpu.HBM)
    query_t = jnp.swapaxes(initial_query, 2, 3)
    dma = pltpu.SemaphoreType.DMA
    merged, basis, w_all, linv = pl.pallas_call(
        reduce_kernel,
        name="reduce",
        out_shape=[
            pltpu.VMEM((LAYERS, 2, ROWS, KVW), BF16),
            pltpu.VMEM((LAYERS, ROWS, 2 * R), BF16),
            pltpu.VMEM((LAYERS, 2, 4, R, 256), BF16),
            pltpu.VMEM((LAYERS, 2, R, 2 * R), F32),
        ],
        in_specs=[hbm, hbm, hbm],
        out_specs=[vmem] * 4,
        scratch_shapes=[
            pltpu.VMEM((LAYERS, 2, ROWS, KVW), BF16),
            pltpu.VMEM((LAYERS, 2, ROWS, KVW), BF16),
            pltpu.VMEM((LAYERS, 2, R, KVW), F32),
            pltpu.VMEM((LAYERS, 2, KVW, 2 * R), BF16),
            pltpu.VMEM((LAYERS, ROWS, 2 * R), F32),
            pltpu.VMEM((LAYERS, ROWS, 2 * R), BF16),
            pltpu.VMEM((LAYERS, 7, 64, 2 * R), BF16),
            pltpu.VMEM((LAYERS, ROWS, 2 * R), BF16),
            pltpu.VMEM((LAYERS, 2 * R, ROWS), BF16),
            pltpu.VMEM((LAYERS, 2, 4, R, 256), BF16),
            pltpu.VMEM((LAYERS, 2, 7, 32, 256), BF16),
            pltpu.VMEM((LAYERS, 2, 4, 32, 256), BF16),
            pltpu.VMEM((LAYERS, 2, 4, 32, 256), BF16),
            pltpu.VMEM((4, 96, 2 * R), F32),
            pltpu.VMEM((4, 96, 2 * R), F32),
            pltpu.VMEM((LAYERS, R, 2 * R), F32),
            dma((LAYERS, 2)),
            dma((LAYERS,)),
            dma((9,)),
            dma((LAYERS, 2)),
            dma((LAYERS, 2, 4)),
            dma((3,)),
            dma,
        ],
        compiler_params=pltpu.CompilerParams(collective_id=0, has_side_effects=True, vmem_limit_bytes=54 << 20),
    )(gradients, memory, query_t)

    new_memory, rebuilt, query = pl.pallas_call(
        functools.partial(rebuild_kernel, replicas),
        name="rebuild",
        out_shape=[
            jax.ShapeDtypeStruct((1, LAYERS, 2, ROWS, KVW), BF16),
            jax.ShapeDtypeStruct((LAYERS, 2, ROWS, KVW), BF16),
            jax.ShapeDtypeStruct((LAYERS, 2, R, KVW), F32),
        ],
        in_specs=[vmem] * 4,
        out_specs=[hbm] * 3,
        scratch_shapes=[
            pltpu.VMEM((LAYERS, 2, 2 * R, KVW), BF16),
            pltpu.VMEM((LAYERS, 2, ROWS, KVW), BF16),
            pltpu.VMEM((LAYERS, 2, ROWS, KVW), BF16),
            pltpu.VMEM((LAYERS, 2, R, KVW), F32),
            dma((3,)),
        ],
        compiler_params=pltpu.CompilerParams(vmem_limit_bytes=36 << 20),
    )(merged, basis, w_all, linv)
    return new_memory, rebuilt, jnp.swapaxes(query, 2, 3)


def solution(mesh):
    in_specs = (P("dp", None, None, "tensor", None), P("dp", None, None, "tensor", None), P())
    out_specs = (P("dp", None, None, "tensor", None), P(None, None, "tensor", None), P())
    return jax.shard_map(body, mesh=mesh, in_specs=in_specs, out_specs=out_specs, check_vma=False)
```

time: 48.3 us -> 47.2 us (0.977)
  Pallas kernels: 47.6 us -> 46.5 us
    pallas_call x1, Pallas kernels: 42.2 us -> 41.1 us  [body(): pl.pallas_call(reduce_kernel, name='reduce', out_shape=[pltpu.VMEM((LAYER...]
where the time goes in v6:
time: 47.2 us; the launch traced here: 47.1 us
  Pallas kernels  46.5 us (99%)
  between operations  0.64 us (1%)
    pallas_call x1, Pallas kernels, body(): pl.pallas_call(reduce_kernel, name='reduce', out_shape=[pltpu.VMEM((LAYER...  41.1 us
    pallas_call x1, Pallas kernels, body(): pl.pallas_call(functools.partial(rebuild_kernel, replicas), name='rebuild...  5.4 us

profile of v6, /device:TPU:1, one launch (start us, length us, event | category | flops | bytes accessed | tf_op | source)
XLA Modules:
  0.0 47.1 jit_solution(13990797552895966749)
XLA Ops:
  0.6 41.1 %reduce.1 = (bf16[3,2,512,1024]{3,2,1,0:T(8,128)(2,1)S(1)}, bf16[3,512,128]{2,1,0:T(8,128)(2,1)S(1)}, bf16[3,2,4,64,256]{4,3,2,1,0:T(8,128)(2,1)S(1)}, f32[3,2,64,128]{3,2,1,0:T(8,128)S(1)}) custom-call(bf16[1,3,2,512,1024]{4,3,2,1,0:T(8,128)(2,1)} %g_hbm.1, bf16[1,3,2,512,1024]{4,3,2,1,0:T(8,128)(2,1)} %m_hbm.1, f32[3,2,64,1024]{3,2,1,0:T(8,128)} %bitcast.2), custom_call_target="tpu_custom_call" | custom-call | tf_op jit(solution)/shard_map/reduce/pallas_call | solution.py:296
  41.7 5.4 %rebuild.1 = (bf16[1,3,2,512,1024]{4,3,2,1,0:T(8,128)(2,1)}, bf16[3,2,512,1024]{3,2,1,0:T(8,128)(2,1)}, f32[3,2,64,1024]{3,2,1,0:T(8,128)}) custom-call(bf16[3,2,512,1024]{3,2,1,0:T(8,128)(2,1)S(1)} %get-tuple-element.10.merged, bf16[3,512,128]{2,1,0:T(8,128)(2,1)S(1)} %get-tuple-element.11.basis, bf16[3,2,4,64,256]{4,3,2,1,0:T(8,128)(2,1)S(1)} %get-tuple-element.12.w_all, ...), custom_call_target="tpu_custom_call" | custom-call | tf_op jit(solution)/shard_map/rebuild/pallas_call | solution.py:335

commit v7 on v6

--- a/solution.py
+++ b/solution.py
@@ -208,13 +208,22 @@
         for b in range(first, end):
             top = [a[0:8] for a in state]
             state = [a[8:] for a in state]
-            for i in range(8):
+            for i in range(0, 8, 2):
                 j = 8 * b + i
                 for l in range(LAYERS):
-                    scaled = top[l][i:i + 1, :] / top[l][i:i + 1, j:j + 1]
-                    top[l] = top[l] - jnp.where(row > i, top[l][:, j:j + 1], 0.0) * scaled
+                    t = top[l]
+                    col, col2 = (jnp.broadcast_to(t[:, n:n + 1], t.shape) for n in (j, j + 1))
+                    inverse = 1.0 / col[i:i + 1]
+                    first = t[i:i + 1] * inverse
+                    u, v = col[i + 1:i + 2] * inverse, col2[i:i + 1] * inverse
+                    second = t[i + 1:i + 2] - u * t[i:i + 1]
+                    scaled = second / (col2[i + 1:i + 2] - u * col2[i:i + 1])
+                    lower = t - col * first - (col2 - col * v) * scaled
+                    top[l] = jnp.where(row > i + 1, lower, jnp.where(row == i + 1, second, t))
                     if j < R - 8:
-                        state[l] = state[l] - state[l][:, j:j + 1] * scaled
+                        t = state[l]
+                        col, col2 = (jnp.broadcast_to(t[:, n:n + 1], t.shape) for n in (j, j + 1))
+                        state[l] = t - col * first - (col2 - col * v) * scaled
             for l in range(LAYERS):
                 aug[l, 8 * b:8 * b + 8, :] = top[l]
         if end < R // 8:
@@ -246,7 +255,7 @@
         (stage_a, 0), (stage_a, 1), (stage_a, 2), (stage_r, 0), (stage_r, 1), (stage_r, 2),
         (stage_d, 0), (stage_d, 1), (gram_a, 0, 64), (stage_d, 2), (gram_a, 64, 32),
         (stage_f, 0), (stage_f, 1), (stage_f, 2), (gram_b,), (stage_h, 0), (stage_h, 1), (stage_h, 2),
-        (gram_c,), (eliminate, 0, 5), (stage_i, 0), (stage_i, 1), (stage_i, 2), (eliminate, 5, 8), (invert,), (gram_d,),
+        (gram_c,), (eliminate, 0, 4), (stage_i, 0), (stage_i, 1), (stage_i, 2), (eliminate, 4, 8), (invert,), (gram_d,),
         (stage_k, 0), (stage_k, 1), (stage_k, 2),
     ]
     for stage in plan:

time: 47.2 us -> 45.1 us (0.956)
  Pallas kernels: 46.5 us -> 44.3 us
    pallas_call x1, Pallas kernels: 41.1 us -> 38.9 us  [body(): pl.pallas_call(reduce_kernel, name='reduce', out_shape=[pltpu.VMEM((LAYER...]
where the time goes in v7:
time: 45.1 us; the launch traced here: 45 us
  Pallas kernels  44.3 us (98%)
  between operations  0.64 us (1%)
    pallas_call x1, Pallas kernels, body(): pl.pallas_call(reduce_kernel, name='reduce', out_shape=[pltpu.VMEM((LAYER...  38.9 us
    pallas_call x1, Pallas kernels, body(): pl.pallas_call(functools.partial(rebuild_kernel, replicas), name='rebuild...  5.4 us

profile of v7, /device:TPU:1, one launch (start us, length us, event | category | flops | bytes accessed | tf_op | source)
XLA Modules:
  0.0 45.0 jit_solution(10244883453820427124)
XLA Ops:
  0.6 38.9 %reduce.1 = (bf16[3,2,512,1024]{3,2,1,0:T(8,128)(2,1)S(1)}, bf16[3,512,128]{2,1,0:T(8,128)(2,1)S(1)}, bf16[3,2,4,64,256]{4,3,2,1,0:T(8,128)(2,1)S(1)}, f32[3,2,64,128]{3,2,1,0:T(8,128)S(1)}) custom-call(bf16[1,3,2,512,1024]{4,3,2,1,0:T(8,128)(2,1)} %g_hbm.1, bf16[1,3,2,512,1024]{4,3,2,1,0:T(8,128)(2,1)} %m_hbm.1, f32[3,2,64,1024]{3,2,1,0:T(8,128)} %bitcast.2), custom_call_target="tpu_custom_call" | custom-call | tf_op jit(solution)/shard_map/reduce/pallas_call | solution.py:305
  39.6 5.4 %rebuild.1 = (bf16[1,3,2,512,1024]{4,3,2,1,0:T(8,128)(2,1)}, bf16[3,2,512,1024]{3,2,1,0:T(8,128)(2,1)}, f32[3,2,64,1024]{3,2,1,0:T(8,128)}) custom-call(bf16[3,2,512,1024]{3,2,1,0:T(8,128)(2,1)S(1)} %get-tuple-element.10.merged, bf16[3,512,128]{2,1,0:T(8,128)(2,1)S(1)} %get-tuple-element.11.basis, bf16[3,2,4,64,256]{4,3,2,1,0:T(8,128)(2,1)S(1)} %get-tuple-element.12.w_all, ...), custom_call_target="tpu_custom_call" | custom-call | tf_op jit(solution)/shard_map/rebuild/pallas_call | solution.py:344

commit v8 on v7

--- a/solution.py
+++ b/solution.py
@@ -16,6 +16,7 @@
 R = 64
 CHUNK = 256
 DEPTH = 4
+ORDERS = (((1, 2, 0), (2, 0, 1)), ((1, 0, 2), (2, 1, 0)), ((0, 1, 2), (2, 0, 1)))
 NT = (((1,), (1,)), ((), ()))
 
 
@@ -129,7 +130,7 @@
                 remote(piece, r1.at[l, h, n], send.at[2], w_arrive.at[l, h, 0], along(axis, k, other))
 
     def axes(l, h):
-        return (l + h) % 3, (l + h + 1) % 3, (l + h + 2) % 3
+        return ORDERS[l][h]
 
     def exchange(slots, l, h, phase, value):
         axis = axes(l, h)[phase]
@@ -253,7 +254,7 @@
 
     plan = [
         (stage_a, 0), (stage_a, 1), (stage_a, 2), (stage_r, 0), (stage_r, 1), (stage_r, 2),
-        (stage_d, 0), (stage_d, 1), (gram_a, 0, 64), (stage_d, 2), (gram_a, 64, 32),
+        (stage_d, 0), (stage_d, 1), (stage_d, 2), (gram_a, 0, 64), (gram_a, 64, 32),
         (stage_f, 0), (stage_f, 1), (stage_f, 2), (gram_b,), (stage_h, 0), (stage_h, 1), (stage_h, 2),
         (gram_c,), (eliminate, 0, 4), (stage_i, 0), (stage_i, 1), (stage_i, 2), (eliminate, 4, 8), (invert,), (gram_d,),
         (stage_k, 0), (stage_k, 1), (stage_k, 2),

time: 45.1 us -> 44.5 us (0.987)
  Pallas kernels: 44.3 us -> 43.8 us
    pallas_call x1, Pallas kernels: 38.9 us -> 38.4 us  [body(): pl.pallas_call(reduce_kernel, name='reduce', out_shape=[pltpu.VMEM((LAYER...]
where the time goes in v8:
time: 44.5 us; the launch traced here: 44.4 us
  Pallas kernels  43.8 us (98%)
  between operations  0.64 us (1%)
    pallas_call x1, Pallas kernels, body(): pl.pallas_call(reduce_kernel, name='reduce', out_shape=[pltpu.VMEM((LAYER...  38.4 us
    pallas_call x1, Pallas kernels, body(): pl.pallas_call(functools.partial(rebuild_kernel, replicas), name='rebuild...  5.4 us

profile of v8, /device:TPU:1, one launch (start us, length us, event | category | flops | bytes accessed | tf_op | source)
XLA Modules:
  0.0 44.4 jit_solution(17206068200753104849)
XLA Ops:
  0.6 38.4 %reduce.1 = (bf16[3,2,512,1024]{3,2,1,0:T(8,128)(2,1)S(1)}, bf16[3,512,128]{2,1,0:T(8,128)(2,1)S(1)}, bf16[3,2,4,64,256]{4,3,2,1,0:T(8,128)(2,1)S(1)}, f32[3,2,64,128]{3,2,1,0:T(8,128)S(1)}) custom-call(bf16[1,3,2,512,1024]{4,3,2,1,0:T(8,128)(2,1)} %g_hbm.1, bf16[1,3,2,512,1024]{4,3,2,1,0:T(8,128)(2,1)} %m_hbm.1, f32[3,2,64,1024]{3,2,1,0:T(8,128)} %bitcast.2), custom_call_target="tpu_custom_call" | custom-call | tf_op jit(solution)/shard_map/reduce/pallas_call | solution.py:306
  39.0 5.4 %rebuild.1 = (bf16[1,3,2,512,1024]{4,3,2,1,0:T(8,128)(2,1)}, bf16[3,2,512,1024]{3,2,1,0:T(8,128)(2,1)}, f32[3,2,64,1024]{3,2,1,0:T(8,128)}) custom-call(bf16[3,2,512,1024]{3,2,1,0:T(8,128)(2,1)S(1)} %get-tuple-element.10.merged, bf16[3,512,128]{2,1,0:T(8,128)(2,1)S(1)} %get-tuple-element.11.basis, bf16[3,2,4,64,256]{4,3,2,1,0:T(8,128)(2,1)S(1)} %get-tuple-element.12.w_all, ...), custom_call_target="tpu_custom_call" | custom-call | tf_op jit(solution)/shard_map/rebuild/pallas_call | solution.py:345

commit v9 on v8

--- a/solution.py
+++ b/solution.py
@@ -31,12 +31,18 @@
     core = dp % 2
     coord = (dp // 2, tensor // 4, tensor % 4)
 
+    cores = (core, 1 - core)
+    ring = {(axis, k): lax.rem(coord[axis] + k, 4) if k else coord[axis] for axis in range(3) for k in range(4)}
+    devices = {}
+    for axis in range(3):
+        for k in range(4):
+            for other in range(2):
+                x, y, z = (ring[axis, k] if a == axis else coord[a] for a in range(3))
+                devices[axis, k, other] = (x * 2 + cores[other], y * 4 + z)
+    sibling = devices[0, 0, 1]
+
     def along(axis, k, other=0):
-        c = [coord[0], coord[1], coord[2]]
-        c[axis] = (c[axis] + k) % 4
-        return (c[0] * 2 + (core + other) % 2, c[1] * 4 + c[2])
-
-    sibling = (dp + 1 - 2 * core, tensor)
+        return devices[axis, k, other]
 
     query_loads = [pltpu.make_async_copy(query_hbm.at[l], query.at[l], query_sem.at[l]) for l in range(LAYERS)]
     loads = [
@@ -103,7 +109,7 @@
         if l == 0:
             pl.semaphore_wait(barrier, 19)
         for n, (k, other) in enumerate(partners):
-            owner = (coord[0] + k) % 4 * 2 + (core + other) % 2
+            owner = ring[0, k] * 2 + cores[other]
             remote(p_send.at[l, row64(owner)], p_part.at[l, n], send.at[0], s_recv.at[l, 0], along(0, k, other))
 
     def stage_r(l):
@@ -126,7 +132,7 @@
         for h in range(2):
             axis = axes(l, h)[0]
             for n, (k, other) in enumerate(partners):
-                piece = w_send.at[l, (core + other) % 2, (coord[axis] + k) % 4, pl.ds(32 * h, 32)]
+                piece = w_send.at[l, cores[other], ring[axis, k], pl.ds(32 * h, 32)]
                 remote(piece, r1.at[l, h, n], send.at[2], w_arrive.at[l, h, 0], along(axis, k, other))
 
     def axes(l, h):

time: 44.5 us -> 44.5 us (level)
  no operation moved by 1% of the time
where the time goes in v9:
time: 44.5 us; the launch traced here: 44.4 us
  Pallas kernels  43.8 us (98%)
  between operations  0.64 us (1%)
    pallas_call x1, Pallas kernels, body(): pl.pallas_call(reduce_kernel, name='reduce', out_shape=[pltpu.VMEM((LAYER...  38.4 us
    pallas_call x1, Pallas kernels, body(): pl.pallas_call(functools.partial(rebuild_kernel, replicas), name='rebuild...  5.4 us

profile of v9, /device:TPU:1, one launch (start us, length us, event | category | flops | bytes accessed | tf_op | source)
XLA Modules:
  0.0 44.4 jit_solution(14194642673076131416)
XLA Ops:
  0.6 38.4 %reduce.1 = (bf16[3,2,512,1024]{3,2,1,0:T(8,128)(2,1)S(1)}, bf16[3,512,128]{2,1,0:T(8,128)(2,1)S(1)}, bf16[3,2,4,64,256]{4,3,2,1,0:T(8,128)(2,1)S(1)}, f32[3,2,64,128]{3,2,1,0:T(8,128)S(1)}) custom-call(bf16[1,3,2,512,1024]{4,3,2,1,0:T(8,128)(2,1)} %g_hbm.1, bf16[1,3,2,512,1024]{4,3,2,1,0:T(8,128)(2,1)} %m_hbm.1, f32[3,2,64,1024]{3,2,1,0:T(8,128)} %bitcast.2), custom_call_target="tpu_custom_call" | custom-call | tf_op jit(solution)/shard_map/reduce/pallas_call | solution.py:312
  39.0 5.4 %rebuild.1 = (bf16[1,3,2,512,1024]{4,3,2,1,0:T(8,128)(2,1)}, bf16[3,2,512,1024]{3,2,1,0:T(8,128)(2,1)}, f32[3,2,64,1024]{3,2,1,0:T(8,128)}) custom-call(bf16[3,2,512,1024]{3,2,1,0:T(8,128)(2,1)S(1)} %get-tuple-element.10.merged, bf16[3,512,128]{2,1,0:T(8,128)(2,1)S(1)} %get-tuple-element.11.basis, bf16[3,2,4,64,256]{4,3,2,1,0:T(8,128)(2,1)S(1)} %get-tuple-element.12.w_all, ...), custom_call_target="tpu_custom_call" | custom-call | tf_op jit(solution)/shard_map/rebuild/pallas_call | solution.py:351

commit v10 on v9

--- a/solution.py
+++ b/solution.py
@@ -15,7 +15,7 @@
 KVW = 1024
 R = 64
 CHUNK = 256
-DEPTH = 4
+DEPTH = 3
 ORDERS = (((1, 2, 0), (2, 0, 1)), ((1, 0, 2), (2, 1, 0)), ((0, 1, 2), (2, 0, 1)))
 NT = (((1,), (1,)), ((), ()))
 
@@ -45,20 +45,14 @@
         return devices[axis, k, other]
 
     query_loads = [pltpu.make_async_copy(query_hbm.at[l], query.at[l], query_sem.at[l]) for l in range(LAYERS)]
-    loads = [
-        (
-            pltpu.make_async_copy(g_hbm.at[0, l, m], g_buf.at[l, m], load_sem.at[l, m]),
-            pltpu.make_async_copy(m_hbm.at[0, l, m], m_buf.at[l, m], load_sem.at[l, m]),
-        )
-        for l in range(LAYERS)
-        for m in range(2)
-    ]
-
     def load(i):
-        if i % 2 == 0:
-            query_loads[i // 2].start()
-        loads[i][0].start()
-        loads[i][1].start()
+        l, m = i // 2, i % 2
+        if m == 0:
+            query_loads[l].start()
+        for n in range(ROWS // CHUNK):
+            rows = pl.ds(n * CHUNK, CHUNK)
+            pltpu.make_async_copy(g_hbm.at[0, l, m, rows], g_buf.at[l, m, rows], load_sem.at[l, m, n]).start()
+            pltpu.make_async_copy(m_hbm.at[0, l, m, rows], m_buf.at[l, m, rows], load_sem.at[l, m, n]).start()
 
     for i in range(DEPTH):
         load(i)
@@ -96,11 +90,11 @@
         right_factor(l)
         for m in range(2):
             i = 2 * l + m
-            drain(g_buf.at[0], load_sem.at[l, m])
-            if i + DEPTH < len(loads):
+            if i + DEPTH < 2 * LAYERS:
                 load(i + DEPTH)
-            for r in range(0, ROWS, CHUNK):
-                rows = slice(r, r + CHUNK)
+            for n in range(ROWS // CHUNK):
+                drain(g_buf.at[0, :, pl.ds(0, CHUNK)], load_sem.at[l, m, n])
+                rows = slice(n * CHUNK, n * CHUNK + CHUNK)
                 block = g_buf[l, m, rows] + m_buf[l, m, rows]
                 merged[l, m, rows] = block
                 part = jnp.dot(block, qpad[l, m], preferred_element_type=F32)
@@ -129,9 +123,9 @@
             w = jnp.dot(s_t[l, R * m:R * m + R, :], merged[l, m], preferred_element_type=F32)
             for j in range(4):
                 w_send[l, m, j] = w[:, 256 * j:256 * j + 256].astype(BF16)
-        for h in range(2):
-            axis = axes(l, h)[0]
-            for n, (k, other) in enumerate(partners):
+        for n, (k, other) in enumerate(partners):
+            for h in range(2):
+                axis = axes(l, h)[0]
                 piece = w_send.at[l, cores[other], ring[axis, k], pl.ds(32 * h, 32)]
                 remote(piece, r1.at[l, h, n], send.at[2], w_arrive.at[l, h, 0], along(axis, k, other))
 
@@ -337,7 +331,7 @@
             pltpu.VMEM((4, 96, 2 * R), F32),
             pltpu.VMEM((4, 96, 2 * R), F32),
             pltpu.VMEM((LAYERS, R, 2 * R), F32),
-            dma((LAYERS, 2)),
+            dma((LAYERS, 2, ROWS // CHUNK)),
             dma((LAYERS,)),
             dma((9,)),
             dma((LAYERS, 2)),

time: 44.5 us -> 44.8 us (level)
  no operation moved by 1% of the time
where the time goes in v10:
time: 44.8 us; the launch traced here: 44.6 us
  Pallas kernels  44 us (98%)
  between operations  0.64 us (1%)
    pallas_call x1, Pallas kernels, body(): pl.pallas_call(reduce_kernel, name='reduce', out_shape=[pltpu.VMEM((LAYER...  38.6 us
    pallas_call x1, Pallas kernels, body(): pl.pallas_call(functools.partial(rebuild_kernel, replicas), name='rebuild...  5.4 us

profile of v10, /device:TPU:1, one launch (start us, length us, event | category | flops | bytes accessed | tf_op | source)
XLA Modules:
  0.0 44.6 jit_solution(3533197403037964024)
XLA Ops:
  0.6 38.6 %reduce.1 = (bf16[3,2,512,1024]{3,2,1,0:T(8,128)(2,1)S(1)}, bf16[3,512,128]{2,1,0:T(8,128)(2,1)S(1)}, bf16[3,2,4,64,256]{4,3,2,1,0:T(8,128)(2,1)S(1)}, f32[3,2,64,128]{3,2,1,0:T(8,128)S(1)}) custom-call(bf16[1,3,2,512,1024]{4,3,2,1,0:T(8,128)(2,1)} %g_hbm.1, bf16[1,3,2,512,1024]{4,3,2,1,0:T(8,128)(2,1)} %m_hbm.1, f32[3,2,64,1024]{3,2,1,0:T(8,128)} %bitcast.2), custom_call_target="tpu_custom_call" | custom-call | tf_op jit(solution)/shard_map/reduce/pallas_call | solution.py:306
  39.2 5.4 %rebuild.1 = (bf16[1,3,2,512,1024]{4,3,2,1,0:T(8,128)(2,1)}, bf16[3,2,512,1024]{3,2,1,0:T(8,128)(2,1)}, f32[3,2,64,1024]{3,2,1,0:T(8,128)}) custom-call(bf16[3,2,512,1024]{3,2,1,0:T(8,128)(2,1)S(1)} %get-tuple-element.10.merged, bf16[3,512,128]{2,1,0:T(8,128)(2,1)S(1)} %get-tuple-element.11.basis, bf16[3,2,4,64,256]{4,3,2,1,0:T(8,128)(2,1)S(1)} %get-tuple-element.12.w_all, ...), custom_call_target="tpu_custom_call" | custom-call | tf_op jit(solution)/shard_map/rebuild/pallas_call | solution.py:345
